TPU v7x, 32 devices: a whole 2x2x4 slice. The times are simulated.
32 devices in a mesh: band: 4 (over x, core), tile: 8 (over z, y).
Axes of the slice: x: 2, y: 2, z: 4, core: 2. Of those that a mesh axis runs over, the one named last changes fastest.
Arguments:
- raw_traces: bfloat16 [8, 1024, 2048], P('tile', 'band'), may hold values from -6 to 6
- bin_owner: int32 [8, 1024, 1], P('tile'), may hold values from 0 to 7; in each aligned block of 1024 rows (0 to 1023, 1024 to 2047, ..., all dimensions but the last counted through in order) at most 256 rows name the same one
- bin_offset: int32 [8, 1024], P('tile'), may hold values from 0 to 32767
Outputs:
- multiples: float32 [40, 2, 512, 512], P('band', None, 'tile')
Inputs may be any that keep to these rules, and one draw needn't show every extreme that they name: `bin_owner`: in each tile's list of 1024 traces at most 256 are binned into one tile, and some tile receives exactly 256.
All inputs are finite; a program needn't handle non-finite values.
Results may differ from a plain program's by a relative error of at most 0.0067.
Values may be sent and summed in bfloat16 or wider, within the bound.
No kernel may reach another device: no remote copies, remote signals or barrier semaphores. Data moves between devices by JAX's collectives and lax.ppermute only.
A program may use at most 128 MiB of HBM per device.

v0:
```python
import math

import jax
import jax.numpy as jnp
from jax import lax
from jax.sharding import PartitionSpec as P

NG = 512
NT = 2048
FB = 10


def twiddle_grid(band_count):
    time_index = jnp.arange(NT, dtype=jnp.int32)
    freq_index = jnp.arange(band_count * FB, dtype=jnp.int32).reshape(band_count, FB) + 1
    phase_angle = (time_index[:, None, None] * freq_index[None, :, :] % NT).astype(jnp.float32) * (
        2.0 * math.pi / NT
    )
    norm_factor = 1.0 / math.sqrt(NT)
    stacked = jnp.stack(
        [jnp.cos(phase_angle) * norm_factor, -jnp.sin(phase_angle) * norm_factor], axis=2
    )
    return stacked.reshape(NT, band_count * 2 * FB).astype(jnp.bfloat16)


def complex_rows(left_rows, right_rows):
    real_real = jnp.einsum(
        "fik,fjk->fij", left_rows[:, 0], right_rows[:, 0], preferred_element_type=jnp.float32
    )
    imag_imag = jnp.einsum(
        "fik,fjk->fij", left_rows[:, 1], right_rows[:, 1], preferred_element_type=jnp.float32
    )
    real_imag = jnp.einsum(
        "fik,fjk->fij", left_rows[:, 0], right_rows[:, 1], preferred_element_type=jnp.float32
    )
    imag_real = jnp.einsum(
        "fik,fjk->fij", left_rows[:, 1], right_rows[:, 0], preferred_element_type=jnp.float32
    )
    return jnp.stack([real_real - imag_imag, real_imag + imag_real], axis=1)


def per_device(raw_traces, bin_owner, bin_offset):
    band_count = lax.axis_size("band")
    tile_count = lax.axis_size("tile")
    traces = raw_traces[0]
    trace_count = traces.shape[0]
    out_scale = 1.0 / math.sqrt(NG)
    twiddle = twiddle_grid(band_count)
    spectra = jnp.dot(traces, twiddle, preferred_element_type=jnp.float32).astype(jnp.bfloat16)
    spectra = spectra.reshape(trace_count, band_count, 2 * FB)
    received = lax.all_to_all(spectra, "band", split_axis=1, concat_axis=0, tiled=True).reshape(
        -1, 2 * FB
    )
    owners = bin_owner[0, :, 0]
    offset = bin_offset[0]
    list_length = owners.shape[0]
    capacity = 2 * list_length // tile_count
    cells_dev = NG * NG // tile_count
    owner_hits = (owners[:, None] == jnp.arange(tile_count, dtype=jnp.int32)[None, :]).astype(
        jnp.int32
    )
    slot_rank = jnp.sum((jnp.cumsum(owner_hits, axis=0) - 1) * owner_hits, axis=1)
    slot_index = owners * capacity + slot_rank
    outgoing = (
        jnp.zeros((2 * FB, tile_count * capacity), jnp.bfloat16).at[:, slot_index].set(received.T)
    )
    outgoing = outgoing.reshape(2 * FB, tile_count, capacity)
    labels = jnp.full((tile_count * capacity,), cells_dev, jnp.int32).at[slot_index].set(offset)
    labels = labels.reshape(tile_count, capacity)
    arrived = lax.all_to_all(outgoing, "tile", split_axis=1, concat_axis=1, tiled=True)
    arrived_cells = lax.all_to_all(labels, "tile", split_axis=0, concat_axis=0, tiled=True).reshape(
        -1
    )
    slot_values = arrived.reshape(2 * FB, -1).T.astype(jnp.float32)
    cell_sums = jax.ops.segment_sum(slot_values, arrived_cells, cells_dev + 1)[:cells_dev]
    counts = jax.ops.segment_sum(
        jnp.ones(arrived_cells.shape, jnp.float32), arrived_cells, cells_dev + 1
    )[:cells_dev]
    grid_field = (cell_sums / jnp.maximum(counts, 1.0)[:, None]).astype(jnp.bfloat16)
    row_block = NG // tile_count
    grid_field = grid_field.T.reshape(2, FB, row_block, NG).transpose(1, 0, 2, 3)
    gathered = lax.all_gather(grid_field, "tile", axis=2, tiled=True)
    symmetric_all = (
        0.5 * (gathered.astype(jnp.float32) + jnp.swapaxes(gathered, 2, 3).astype(jnp.float32))
    ).astype(jnp.bfloat16)
    first_row = lax.axis_index("tile") * row_block
    symmetric = lax.dynamic_slice_in_dim(symmetric_all, first_row, row_block, 2)
    result = complex_rows(symmetric, symmetric_all) * out_scale
    return result


def solution(mesh):
    return jax.shard_map(
        per_device,
        mesh=mesh,
        in_specs=(P("tile", "band", None), P("tile", None, None), P("tile", None)),
        out_specs=P("band", None, "tile", None),
        check_vma=False,
    )
```

profile of v0, /device:TPU:0, one launch (start us, length us, event | category | flops | bytes accessed | tf_op | source)
XLA Modules:
  0.0 321.7 jit_solution(8473244270539582649)
XLA Ops:
  6.5 0.8 fusion.28
  7.3 2.3 reduce-window.6
  10.1 0.7 fusion.27
  10.8 0.7 compare_select_fusion
  11.5 5.0 %scatter_custom_fusion = s32[2048]{0:T(1024)} fusion(s32[1024]{0:T(1024)S(1)} %bitcast.102, s32[1024]{0:T(1024)} %bitcast.104, s32[]{:T(128)} %constant.19.clone.1), kind=kCustom, calls=%fused_computation.56 | custom fusion | bytes 8704 | tf_op jit(solution)/shard_map/scatter | solution.py:68
  16.6 7.3 %all-to-all-start = ((s32[8,1,256]{2,1,0:T(1,128)}), s32[8,1,256]{2,1,0:T(1,128)S(1)}, u32[]{:S(2)}, u32[]{:S(2)}) async-start(s32[8,1,256]{2,1,0:T(1,128)} %bitcast.7), calls=%async_computation | async-start | bytes 16384 | tf_op jit(solution)/shard_map/all_to_all | solution.py:71
  23.8 2.5 multiply_convert_fusion.1
  26.5 0.4 fusion.14
  27.0 0.6 reshape.161
  27.6 2.7 all-to-all-done
  30.3 3.3 %all-to-all-start.1 = ((bf16[256,4,20]{0,2,1:T(8,128)(2,1)}), bf16[256,4,20]{0,2,1:T(8,128)(2,1)S(1)}, u32[]{:S(2)}, u32[]{:S(2)}) async-start(bf16[256,4,20]{0,2,1:T(8,128)(2,1)} %reshape.161), calls=%async_computation.1 | async-start | bytes 98304 | tf_op jit(solution)/shard_map/all_to_all | solution.py:51
  33.6 13.2 %scatter_custom_fusion.3 = f32[32769]{0:T(1024)S(1)} fusion(s32[2048]{0:T(1024)S(1)} %bitcast.100, f32[2048]{0:T(1024)S(1)} %broadcast.167, f32[]{:T(128)} %constant.18.clone.1), kind=kCustom, calls=%fused_computation.44 | custom fusion | flops 2048 | bytes 131080 | tf_op jit(solution)/shard_map/scatter-add | solution.py:76
  47.0 3.3 %scatter_custom_fusion.1 = bf16[20,2048]{0,1:T(8,128)(2,1)S(1)} fusion(s32[1024]{0:T(1024)S(1)} %bitcast.103, bf16[1024,20]{1,0:T(8,128)(2,1)S(1)} %bitcast.94, bf16[]{:T(256)} %constant.14.clone.1), kind=kCustom, calls=%fused_computation.40 | custom fusion | bytes 81922 | tf_op jit(solution)/shard_map/scatter | solution.py:65
  50.4 0.9 copy.37
  51.2 3.4 %all-to-all-start.2 = ((bf16[20,8,256]{2,0,1:T(8,128)(2,1)}), bf16[20,8,256]{2,0,1:T(8,128)(2,1)S(1)}, u32[]{:S(2)}, u32[]{:S(2)}) async-start(bf16[20,8,256]{2,0,1:T(8,128)(2,1)} %copy.37), calls=%async_computation.2 | async-start | bytes 196608 | tf_op jit(solution)/shard_map/all_to_all | solution.py:70
  54.7 7.3 %all-to-all-done.2 = bf16[20,8,256]{2,0,1:T(8,128)(2,1)S(1)} async-done(((bf16[20,8,256]{2,0,1:T(8,128)(2,1)}), bf16[20,8,256]{2,0,1:T(8,128)(2,1)S(1)}, u32[]{:S(2)}, u32[]{:S(2)}) %all-to-all-start.2) | async-done | bytes 81952 | tf_op jit(solution)/shard_map/all_to_all | solution.py:70
  62.1 0.4 copy.39
  62.4 19.9 %scatter_custom_fusion.2 = f32[32769,20]{1,0:T(8,128)} fusion(s32[2048]{0:T(1024)S(1)} %bitcast.101, f32[2048,20]{1,0:T(8,128)S(1)} %copy.39, f32[]{:T(128)} %constant.18.clone.1), kind=kCustom, calls=%fused_computation.9 | custom fusion | flops 40960 | bytes 2621524 | tf_op jit(solution)/shard_map/scatter-add | solution.py:75
  82.3 10.7 %fusion.5 = bf16[20,32768]{0,1:T(8,128)(2,1)} fusion(f32[32768]{0:T(1024)S(1)} %slice_maximum_fusion, f32[32769,20]{1,0:T(8,128)} %scatter_custom_fusion.2), kind=kLoop, calls=%fused_computation.11 | loop fusion | flops 1310720 | bytes 4063232 | tf_op jit(solution)/shard_map/transpose | solution.py:81
  93.0 7.4 %copy.40 = bf16[20,32768]{1,0:T(8,128)(2,1)S(1)} copy(bf16[20,32768]{0,1:T(8,128)(2,1)} %fusion.5) | data formatting | bytes 2621440 | tf_op jit(solution)/shard_map/transpose | solution.py:81
  100.4 0.5 copy.49
  101.1 2.4 copy.41
  103.5 149.0 %all-gather.2.cloned.1.call-done = bf16[10,2,512,512]{3,1,0,2:T(2,128)(2,1)} async-done(((bf16[10,2,64,512]{3,1,0,2:T(2,128)(2,1)}), bf16[10,2,512,512]{3,1,0,2:T(2,128)(2,1)}) %all-gather.2.cloned.1.call-update) | async-done | bytes 10485776 | tf_op jit(solution)/shard_map/all_gather | solution.py:82
  252.5 26.0 %copy.42 = bf16[10,2,512,512]{2,3,0,1:T(8,128)(2,1)} copy(bf16[10,2,512,512]{3,1,0,2:T(2,128)(2,1)} %all-gather.2.cloned.1.call-done) | data formatting | bytes 20971520 | tf_op jit(solution)/shard_map/all_gather | solution.py:82
  278.4 16.3 %copy.43 = f32[10,2,512,512]{3,2,0,1:T(8,128)} copy(bf16[10,2,512,512]{2,3,0,1:T(8,128)(2,1)} %copy.42) | data formatting | bytes 31457280 | tf_op jit(solution)/shard_map/convert_element_type | solution.py:84
  294.8 11.2 %fusion.1 = bf16[10,2,512,512]{3,2,0,1:T(8,128)(2,1)S(1)} fusion(f32[10,2,512,512]{3,2,0,1:T(8,128)} %copy.43, bf16[10,2,512,512]{2,3,0,1:T(8,128)(2,1)} %copy.42), kind=kLoop, calls=%fused_computation.6 | loop fusion | flops 20971520 | bytes 41943040 | tf_op jit(solution)/shard_map/convert_element_type | solution.py:85
  306.0 1.7 fusion.7
  307.7 1.7 fusion.6
  309.4 1.7 fusion.11
  311.1 1.7 fusion.13
  312.8 0.3 maximum_multiply_fusion
  313.1 1.7 copy.44
  (20 shorter events, 1.2 us)
Async XLA Ops:
  6.5 20.0 %copy-start = (bf16[1,256,2048]{2,1,0:T(8,128)(2,1)S(1)}, bf16[1,256,2048]{2,1,0:T(8,128)(2,1)}, u32[]{:S(2)}) copy-start(bf16[1,256,2048]{2,1,0:T(8,128)(2,1)} %param.3) | copy-start | bytes 3145732
  16.6 13.8 %all-to-all-start = ((s32[8,1,256]{2,1,0:T(1,128)}), s32[8,1,256]{2,1,0:T(1,128)S(1)}, u32[]{:S(2)}, u32[]{:S(2)}) async-start(s32[8,1,256]{2,1,0:T(1,128)} %bitcast.7), calls=%async_computation | async-start | bytes 16384 | tf_op jit(solution)/shard_map/all_to_all | solution.py:71
  30.3 16.5 %all-to-all-start.1 = ((bf16[256,4,20]{0,2,1:T(8,128)(2,1)}), bf16[256,4,20]{0,2,1:T(8,128)(2,1)S(1)}, u32[]{:S(2)}, u32[]{:S(2)}) async-start(bf16[256,4,20]{0,2,1:T(8,128)(2,1)} %reshape.161), calls=%async_computation.1 | async-start | bytes 98304 | tf_op jit(solution)/shard_map/all_to_all | solution.py:51
  51.2 10.7 %all-to-all-start.2 = ((bf16[20,8,256]{2,0,1:T(8,128)(2,1)}), bf16[20,8,256]{2,0,1:T(8,128)(2,1)S(1)}, u32[]{:S(2)}, u32[]{:S(2)}) async-start(bf16[20,8,256]{2,0,1:T(8,128)(2,1)} %copy.37), calls=%async_computation.2 | async-start | bytes 196608 | tf_op jit(solution)/shard_map/all_to_all | solution.py:70
  54.6 197.8 %all-gather.2.cloned.1.call-start = ((), (), s32[]{:S(2)}) async-start(), calls=%async_computation.3 | async-start | bytes 11796480 | tf_op jit(solution)/shard_map/all_gather | solution.py:82
  309.4 5.5 %copy-start.1 = (bf16[1,256,2048]{2,1,0:T(8,128)(2,1)S(1)}, bf16[1,256,2048]{2,1,0:T(8,128)(2,1)}, u32[]{:S(2)}) copy-start(bf16[1,256,2048]{2,1,0:T(8,128)(2,1)} %param.3) | copy-start | bytes 3145732
Sparse Core Ops, SparseCore 0:
  103.6 148.7 all-gather.1
where the time goes:
time: 324 us; the launch traced here: 322 us
  waiting for transfers between devices  159 us (49%)
  local copies, waits for them, and re-layouts  65.4 us (20%)
  other arithmetic  62.5 us (19%)
  starting transfers between devices  14 us (4%)
  between operations  13.6 us (4%)
  matrix products  7.21 us (2%)
    all_gather x1, waiting for transfers between devices, per_device(): gathered = lax.all_gather(grid_field, 'tile', axis=2, tiled=True)  149 us
    all_gather x1, local copies, waits for them, and re-layouts, per_device(): gathered = lax.all_gather(grid_field, 'tile', axis=2, tiled=True)  26 us
    scatter-add x1, other arithmetic, per_device(): jax.ops.segment_sum(slot_values, arrived_cells, cells_dev + 1)[:cells_dev]  19.9 us
    convert_element_type x1, local copies, waits for them, and re-layouts, per_device(): gathered.astype(jnp.float32)  16.3 us
    scatter-add x1, other arithmetic, per_device(): jax.ops.segment_sum(jnp.ones(arrived_cells.shape, jnp.float32), arrived_c...  13.2 us
    convert_element_type x1, other arithmetic, per_device(): symmetric_all = (0.5 * (gathered.astype(jnp.float32) + jnp.swapaxes(gathe...  11.2 us
    transpose x1, other arithmetic, per_device(): grid_field.T.reshape(2, FB, row_block, NG).transpose(1, 0, 2, 3)  10.7 us
    transpose x2, local copies, waits for them, and re-layouts, per_device(): grid_field.T.reshape(2, FB, row_block, NG).transpose(1, 0, 2, 3)  9.82 us
  transfers between devices with their start and end apart: 4, of which 3 were waited for; matrix products, arithmetic and copies ran while one was open for 5% of the time, Pallas kernels for 0%

commit v1 on v0

v1 whole, which is shorter than its diff:
```python
import functools
import math

import jax
import jax.numpy as jnp
import ml_dtypes
import numpy as np
from jax import lax
from jax.experimental import pallas as pl
from jax.experimental.pallas import tpu as pltpu
from jax.sharding import PartitionSpec as P

NG = 512
NT = 2048
FB = 10
CH = 2 * FB
ROWS = 32
BLOCK = 16
BLOCKS = NG // BLOCK
WIN = 128
STEP = 4
VMEM = 56 * 1024 * 1024


def twiddle_rows(band_count):
    time_index = np.arange(NT)[None, None, :]
    freq_index = np.arange(band_count * FB).reshape(band_count, FB, 1) + 1
    angle = (time_index * freq_index % NT) * (2.0 * math.pi / NT)
    norm = 1.0 / math.sqrt(NT)
    table = np.zeros((band_count, ROWS, NT), np.float64)
    table[:, :FB] = np.cos(angle) * norm
    table[:, FB:CH] = -np.sin(angle) * norm
    return table.reshape(band_count * ROWS, NT).astype(ml_dtypes.bfloat16)


def contract_last(left, right):
    return lax.dot_general(
        left, right, (((1,), (1,)), ((), ())), preferred_element_type=jnp.float32
    )


def rank_kernel(cells_dev, owner_ref, offset_ref, rank_ref, keys_ref, starts_ref, order, column):
    length = owner_ref.shape[1]
    cell = owner_ref[...] * cells_dev + offset_ref[...]
    place = lax.broadcasted_iota(jnp.int32, (1, length), 1)
    order[...] = cell * length + place
    for first in range(0, length, 128):
        column[first : first + 128, :] = jnp.transpose(
            jnp.broadcast_to(order[:, first : first + 128], (128, 128))
        )
    bound = jnp.minimum(lax.broadcasted_iota(jnp.int32, (1, 128), 1), BLOCKS)
    limit = bound * (BLOCK * NG * length)

    def below(bound):
        hits = (column[...] < bound).astype(jnp.int32)
        return jnp.sum(hits, axis=0, keepdims=True)

    starts_ref[...] = below(limit)

    def one(block, _):
        lanes = pl.ds(pl.multiple_of(block * 128, 128), 128)
        rank_ref[:, lanes] = below(order[:, lanes])
        return 0

    lax.fori_loop(0, length // 128, one, 0)
    source = cell // NG
    receiver = cell % NG
    row = lax.broadcasted_iota(jnp.int32, (ROWS, length), 0)
    digits = jnp.where(row == CH, source // BLOCK, 0)
    digits = jnp.where(row == CH + 1, source % BLOCK, digits)
    digits = jnp.where(row == CH + 2, receiver // 256, digits)
    digits = jnp.where(row == CH + 3, receiver % 256, digits)
    keys_ref[...] = digits.astype(jnp.float32).astype(jnp.bfloat16)


def sort_kernel(values_ref, rank_ref, keys_ref, sorted_ref, held):
    parts, _, width = values_ref.shape
    length = parts * width
    for part in range(parts):
        held[:, part * width : (part + 1) * width] = (
            values_ref[part] + keys_ref[:, part * width : (part + 1) * width]
        )
    size = 256
    rank = rank_ref[...]

    def one(block, _):
        first = pl.multiple_of(block * size, size)
        target = lax.broadcasted_iota(jnp.int32, (size, length), 0) + first
        permute = (target == rank).astype(jnp.float32).astype(jnp.bfloat16)
        sorted_ref[:, pl.ds(first, size)] = contract_last(held[...], permute).astype(
            jnp.bfloat16
        )
        return 0

    lax.fori_loop(0, length // size, one, 0)


def list_kernel(windows, starts_ref, list_ref, steps_ref):
    runs = starts_ref.shape[0]

    def block(b, _):
        def run(r, filled):
            start = starts_ref[r, b]
            end = starts_ref[r, b + 1]
            first = start // WIN
            last = jnp.where(end > start, (end + WIN - 1) // WIN, first)

            def window(w, at):
                list_ref[b, at] = r * windows + w
                return at + 1

            return lax.fori_loop(first, last, window, filled)

        filled = lax.fori_loop(0, runs, run, 0)
        steps = (filled + STEP - 1) // STEP

        def pad(at, _):
            list_ref[b, at] = -1
            return 0

        lax.fori_loop(filled, steps * STEP, pad, 0)
        steps_ref[b, 0] = steps
        return 0

    lax.fori_loop(0, BLOCKS, block, 0)


def grid_kernel(
    scale, row_block, list_ref, steps_ref, tile_ref, lists_ref, out_ref, grid, left, right, total, turned
):
    windows = lists_ref.shape[2] // WIN
    lane_row = lax.broadcasted_iota(jnp.int32, (BLOCK, WIN), 0).astype(jnp.float32)
    lane_col = lax.broadcasted_iota(jnp.int32, (NG, WIN), 0).astype(jnp.float32)

    def block(b, _):
        total[...] = jnp.zeros_like(total)

        def step(i, _):
            for q in range(STEP):
                entry = list_ref[b, i * STEP + q]
                wanted = jnp.where(entry < 0, -1, b).astype(jnp.float32)
                entry = jnp.maximum(entry, 0)
                run = entry // windows
                first = pl.multiple_of((entry % windows) * WIN, WIN)
                part = lists_ref[run, :, pl.ds(first, WIN)].astype(jnp.float32)
                hit = (part[CH : CH + 1] == wanted) & (part[CH + 1 : CH + 2] == lane_row)
                cols = slice(q * WIN, (q + 1) * WIN)
                for c in range(CH):
                    left[c * BLOCK : (c + 1) * BLOCK, cols] = jnp.where(
                        hit, part[c : c + 1], 0.0
                    ).astype(jnp.bfloat16)
                left[CH * BLOCK :, cols] = jnp.where(hit, 1.0, 0.0).astype(jnp.bfloat16)
                receiver = part[CH + 2 : CH + 3] * 256.0 + part[CH + 3 : CH + 4]
                right[:, cols] = jnp.where(receiver == lane_col, 1.0, 0.0).astype(jnp.bfloat16)
            total[...] += contract_last(left[...], right[...])
            return 0

        lax.fori_loop(0, steps_ref[b, 0], step, 0)
        inverse = 1.0 / jnp.maximum(total[CH * BLOCK :, :], 1.0)
        rows = pl.ds(pl.multiple_of(b * BLOCK, BLOCK), BLOCK)
        for c in range(CH):
            grid[c, rows, :] = (total[c * BLOCK : (c + 1) * BLOCK, :] * inverse).astype(
                jnp.bfloat16
            )
        return 0

    lax.fori_loop(0, BLOCKS, block, 0)

    first_row = pl.multiple_of(tile_ref[0] * row_block, row_block)
    first_col = pl.multiple_of(first_row // 128 * 128, 128)
    within = pl.multiple_of(first_row % 128, row_block)

    def own_rows(c):
        turned[...] = jnp.transpose(grid[c, :, pl.ds(first_col, 128)].astype(jnp.float32))
        across = turned[pl.ds(within, row_block), :]
        along = grid[c, pl.ds(first_row, row_block), :].astype(jnp.float32)
        return (0.5 * (along + across)).astype(jnp.bfloat16)

    def frequency(f, _):
        own = jnp.concatenate([own_rows(f), own_rows(FB + f)], axis=0)
        real = grid[f]
        imag = grid[FB + f]
        by_real = jnp.dot(own, real, preferred_element_type=jnp.float32) + contract_last(own, real)
        by_imag = jnp.dot(own, imag, preferred_element_type=jnp.float32) + contract_last(own, imag)
        half = 0.5 * scale
        out_ref[f, 0] = (by_real[:row_block] - by_imag[row_block:]) * half
        out_ref[f, 1] = (by_imag[:row_block] + by_real[row_block:]) * half
        return 0

    lax.fori_loop(0, FB, frequency, 0)


def whole(space=pltpu.VMEM):
    return pl.BlockSpec(memory_space=space)


def per_device(raw_traces, bin_owner, bin_offset):
    band_count = lax.axis_size("band")
    tile_count = lax.axis_size("tile")
    length = bin_offset.shape[1]
    cells_dev = NG * NG // tile_count
    row_block = NG // tile_count
    windows = length // WIN
    params = pltpu.CompilerParams(vmem_limit_bytes=VMEM)

    rank, keys, starts = pl.pallas_call(
        functools.partial(rank_kernel, cells_dev),
        out_shape=[
            jax.ShapeDtypeStruct((1, length), jnp.int32),
            jax.ShapeDtypeStruct((ROWS, length), jnp.bfloat16),
            jax.ShapeDtypeStruct((1, 128), jnp.int32),
        ],
        in_specs=[whole()] * 2,
        out_specs=[whole()] * 3,
        scratch_shapes=[
            pltpu.VMEM((1, length), jnp.int32),
            pltpu.VMEM((length, 128), jnp.int32),
        ],
        compiler_params=params,
        name="rank",
    )(bin_owner.reshape(1, length), bin_offset)
    starts_all = lax.all_gather(starts, "tile", axis=0, tiled=True)

    spectra = contract_last(jnp.asarray(twiddle_rows(band_count)), raw_traces[0]).astype(
        jnp.bfloat16
    )
    spectra = spectra.reshape(band_count, ROWS, -1)
    received = lax.all_to_all(spectra, "band", split_axis=0, concat_axis=0, tiled=True)
    ordered = pl.pallas_call(
        sort_kernel,
        out_shape=jax.ShapeDtypeStruct((ROWS, length), jnp.bfloat16),
        in_specs=[whole()] * 3,
        out_specs=whole(),
        scratch_shapes=[pltpu.VMEM((ROWS, length), jnp.bfloat16)],
        compiler_params=params,
        name="sort",
    )(received, rank, keys)
    lists = lax.all_gather(ordered[None], "tile", axis=0, tiled=True)

    most = tile_count * windows + STEP
    window_list, steps = pl.pallas_call(
        functools.partial(list_kernel, windows),
        out_shape=[
            jax.ShapeDtypeStruct((BLOCKS, most), jnp.int32),
            jax.ShapeDtypeStruct((BLOCKS, 1), jnp.int32),
        ],
        in_specs=[whole(pltpu.SMEM)],
        out_specs=[whole(pltpu.SMEM)] * 2,
        compiler_params=params,
        name="windows",
    )(starts_all)

    tile = lax.axis_index("tile").astype(jnp.int32).reshape(1)
    return pl.pallas_call(
        functools.partial(grid_kernel, 1.0 / math.sqrt(NG), row_block),
        out_shape=jax.ShapeDtypeStruct((FB, 2, row_block, NG), jnp.float32),
        in_specs=[whole(pltpu.SMEM)] * 3 + [whole()],
        out_specs=whole(),
        scratch_shapes=[
            pltpu.VMEM((CH, NG, NG), jnp.bfloat16),
            pltpu.VMEM(((CH + 1) * BLOCK, STEP * WIN), jnp.bfloat16),
            pltpu.VMEM((NG, STEP * WIN), jnp.bfloat16),
            pltpu.VMEM(((CH + 1) * BLOCK, NG), jnp.float32),
            pltpu.VMEM((128, NG), jnp.float32),
        ],
        compiler_params=params,
        name="grid",
    )(window_list, steps, tile, lists)


def solution(mesh):
    return jax.shard_map(
        per_device,
        mesh=mesh,
        in_specs=(P("tile", "band", None), P("tile", None, None), P("tile", None)),
        out_specs=P("band", None, "tile", None),
        check_vma=False,
    )
```

time: 324 us -> 130 us (0.40)
  waiting for transfers between devices: 159 us -> 0.01 us
  Pallas kernels: 0 us -> 65.5 us
  local copies, waits for them, and re-layouts: 65.4 us -> 1.83 us
  other arithmetic: 62.5 us -> 0 us
  blocking collectives: 0 us -> 55.4 us
  between operations: 13.6 us -> 0.03 us
  starting transfers between devices: 14 us -> 4.21 us
  matrix products: 7.21 us -> 2.14 us
    all_gather x1 -> x0, waiting for transfers between devices: 149 us -> none  [per_device(): gathered = lax.all_gather(grid_field, 'tile', axis=2, tiled=True)]
    pallas_call x0 -> x4, Pallas kernels: none -> 65.5 us  [the longest x1 49.9 us: per_device(): pl.pallas_call(functools.partial(grid_kernel, 1.0 / math.sqrt(NG), row_bl...]
    all_gather x0 -> x2, blocking collectives: none -> 55.4 us  [the longest x1 33.6 us: per_device(): lists = lax.all_gather(ordered[None], 'tile', axis=0, tiled=True)]
    scatter-add x2 -> x0, other arithmetic: 33.1 us -> none  [the longest x1 19.9 us: per_device(): jax.ops.segment_sum(slot_values, arrived_cells, cells_dev + 1)[:cells_dev]]
    all_gather x1 -> x0, local copies, waits for them, and re-layouts: 26 us -> none  [per_device(): gathered = lax.all_gather(grid_field, 'tile', axis=2, tiled=True)]
    convert_element_type x3 -> x0, local copies, waits for them, and re-layouts: 16.8 us -> none  [the longest x1 16.3 us: per_device(): gathered.astype(jnp.float32)]
    convert_element_type x3 -> x0, other arithmetic: 12 us -> none  [the longest x1 11.2 us: per_device(): symmetric_all = (0.5 * (gathered.astype(jnp.float32) + jnp.swapaxes(gathe...]
    transpose x1 -> x0, other arithmetic: 10.7 us -> none  [per_device(): grid_field.T.reshape(2, FB, row_block, NG).transpose(1, 0, 2, 3)]
  transfers between devices with their start and end apart: 4 -> 1, of which waited for: 3 -> 0; matrix products, arithmetic and copies ran while one was open for 5% -> 0% of each run, Pallas kernels for 0% -> 10%
where the time goes in v1:
time: 130 us; the launch traced here: 129 us
  Pallas kernels  65.5 us (50%)
  blocking collectives  55.4 us (43%)
  starting transfers between devices  4.21 us (3%)
  matrix products  2.14 us (2%)
  local copies, waits for them, and re-layouts  1.83 us (1%)
    pallas_call x1, Pallas kernels, per_device(): pl.pallas_call(functools.partial(grid_kernel, 1.0 / math.sqrt(NG), row_bl...  49.9 us
    all_gather x1, blocking collectives, per_device(): lists = lax.all_gather(ordered[None], 'tile', axis=0, tiled=True)  33.6 us
    all_gather x1, blocking collectives, per_device(): starts_all = lax.all_gather(starts, 'tile', axis=0, tiled=True)  21.8 us
    pallas_call x1, Pallas kernels, per_device(): pl.pallas_call(functools.partial(list_kernel, windows), out_shape=[jax.Sh...  10.3 us
    all_to_all x1, starting transfers between devices, per_device(): lax.all_to_all(spectra, 'band', split_axis=0, concat_axis=0, tiled=True)  4.21 us
    pallas_call x1, Pallas kernels, per_device(): pl.pallas_call(functools.partial(rank_kernel, cells_dev), out_shape=[jax....  2.69 us
    pallas_call x1, Pallas kernels, per_device(): pl.pallas_call(sort_kernel, out_shape=jax.ShapeDtypeStruct((ROWS, length)...  2.61 us
  transfers between devices with their start and end apart: 1, of which 0 were waited for; matrix products, arithmetic and copies ran while one was open for 0% of the time, Pallas kernels for 10%

profile of v1, /device:TPU:0, one launch (start us, length us, event | category | flops | bytes accessed | tf_op | source)
XLA Modules:
  0.0 129.1 jit_solution(17013451823151999425)
XLA Ops:
  0.0 0.0 copy-start
  0.0 1.2 copy-done
  1.2 2.1 %convolution_convert_fusion = bf16[128,256]{1,0:T(8,128)(2,1)} fusion(bf16[128,2048]{1,0:T(8,128)(2,1)} %constant.6.clone, bf16[1,256,2048]{2,1,0:T(8,128)(2,1)S(1)} %copy-done), kind=kOutput, calls=%fused_computation | convolution fusion | flops 134250496 | bytes 1638400 | tf_op jit(solution)/shard_map/dot_general | solution.py:37
  3.4 4.2 %all-to-all-start = ((bf16[4,32,256]{2,1,0:T(8,128)(2,1)}), bf16[4,32,256]{2,1,0:T(8,128)(2,1)S(1)}, u32[]{:S(2)}, u32[]{:S(2)}) async-start(bf16[4,32,256]{2,1,0:T(8,128)(2,1)} %bitcast.5), calls=%async_computation | async-start | bytes 131072 | tf_op jit(solution)/shard_map/all_to_all | solution.py:228
  7.6 2.7 %rank.1 = (s32[1,1024]{1,0:T(1,128)}, bf16[32,1024]{1,0:T(8,128)(2,1)}, s32[1,128]{1,0:T(1,128)}) custom-call(s32[1,1024]{1,0:T(1,128)} %bitcast.12, s32[1,1024]{1,0:T(1,128)} %offset_ref.1), custom_call_target="tpu_custom_call" | custom-call | tf_op jit(solution)/shard_map/rank/pallas_call | solution.py:206
  10.3 21.8 %all-gather.1 = s32[8,1,128]{2,1,0:T(1,128)} all-gather(s32[1,1,128]{2,1,0:T(1,128)} %bitcast.13), channel_id=1, replica_groups=mesh['band'=4,'tile'=8] {'tile'}, dimensions={0}, use_global_device_ids=true | all-gather | bytes 4608 | tf_op jit(solution)/shard_map/all_gather | solution.py:222
  32.0 10.3 %windows.1 = (s32[32,68]{1,0:T(8,128)}, s32[32,1]{1,0:T(8,128)}) custom-call(s32[8,128]{1,0:T(8,128)} %bitcast.11), custom_call_target="tpu_custom_call" | custom-call | tf_op jit(solution)/shard_map/windows/pallas_call | solution.py:241
  42.4 0.0 all-to-all-done.values_ref
  42.4 0.0 copy-start.1
  42.4 0.6 copy-done.1
  43.0 2.6 %sort.1 = bf16[32,1024]{1,0:T(8,128)(2,1)} custom-call(bf16[4,32,256]{2,1,0:T(8,128)(2,1)} %copy-done.1, s32[1,1024]{1,0:T(1,128)} %get-tuple-element.13.rank_ref, bf16[32,1024]{1,0:T(8,128)(2,1)} %get-tuple-element.14.keys_ref), custom_call_target="tpu_custom_call" | custom-call | tf_op jit(solution)/shard_map/sort/pallas_call | solution.py:229
  45.6 33.6 %all-gather = bf16[256,1024]{1,0:T(8,128)(2,1)} all-gather(bf16[32,1024]{1,0:T(8,128)(2,1)} %sort.1), channel_id=2, replica_groups=mesh['band'=4,'tile'=8] {'tile'}, dimensions={0}, use_global_device_ids=true | all-gather | bytes 589824 | tf_op jit(solution)/shard_map/all_gather | solution.py:238
  79.2 49.9 %grid.1 = f32[10,2,64,512]{3,2,1,0:T(8,128)} custom-call(s32[32,68]{1,0:T(8,128)} %get-tuple-element.11.list_ref, s32[32,1]{1,0:T(8,128)} %get-tuple-element.12.steps_ref, s32[1]{0:T(128)} %bitcast.3.tile_ref, bf16[8,32,1024]{2,1,0:T(8,128)(2,1)} %bitcast.10), custom_call_target="tpu_custom_call" | custom-call | tf_op jit(solution)/shard_map/grid/pallas_call | solution.py:254
Async XLA Ops:
  0.0 1.2 copy-start
  3.4 39.0 %all-to-all-start = ((bf16[4,32,256]{2,1,0:T(8,128)(2,1)}), bf16[4,32,256]{2,1,0:T(8,128)(2,1)S(1)}, u32[]{:S(2)}, u32[]{:S(2)}) async-start(bf16[4,32,256]{2,1,0:T(8,128)(2,1)} %bitcast.5), calls=%async_computation | async-start | bytes 131072 | tf_op jit(solution)/shard_map/all_to_all | solution.py:228
  42.4 0.6 copy-start.1

commit v2 on v0

v2 whole, which is shorter than its diff:
```python
import functools
import math

import jax
import jax.numpy as jnp
import ml_dtypes
import numpy as np
from jax import lax
from jax.experimental import pallas as pl
from jax.experimental.pallas import tpu as pltpu
from jax.sharding import PartitionSpec as P

NG = 512
NT = 2048
FB = 10
CH = 2 * FB
ROWS = 24
BLOCK = 16
BLOCKS = NG // BLOCK
GROUP = 32
COPY = 32
CHUNK = 256
UNROLL = 2
VMEM = 56 * 1024 * 1024


def twiddle_rows(band_count):
    time_index = np.arange(NT)[None, None, :]
    freq_index = np.arange(band_count * FB).reshape(band_count, FB, 1) + 1
    angle = (time_index * freq_index % NT) * (2.0 * math.pi / NT)
    norm = 1.0 / math.sqrt(NT)
    table = np.zeros((band_count, ROWS, NT), np.float64)
    table[:, :FB] = np.cos(angle) * norm
    table[:, FB:CH] = -np.sin(angle) * norm
    return table.reshape(band_count * ROWS, NT).astype(ml_dtypes.bfloat16)


def contract_last(left, right):
    return lax.dot_general(
        left, right, (((1,), (1,)), ((), ())), preferred_element_type=jnp.float32
    )


def run_kernel(cells_dev, twiddle_ref, traces_ref, owner_ref, offset_ref, out_ref):
    bands, tiles, _, count = out_ref.shape
    lanes = pl.ds(pl.multiple_of(lax.axis_index("band") * count, count), count)
    cell = owner_ref[:, lanes] * cells_dev + offset_ref[:, lanes]
    order = cell * count + lax.broadcasted_iota(jnp.int32, (1, count), 1)
    rank = jnp.zeros((1, count), jnp.int32)
    for first in range(0, count, 128):
        column = jnp.transpose(jnp.broadcast_to(order[:, first : first + 128], (128, 128)))
        column = jnp.concatenate([column] * (count // 128), axis=1)
        rank += jnp.sum((column < order).astype(jnp.int32), axis=0, keepdims=True)
    target = lax.broadcasted_iota(jnp.int32, (count, count), 0)
    permute = (target == rank).astype(jnp.float32).astype(jnp.bfloat16)
    source = cell // NG
    receiver = cell % NG
    row = lax.broadcasted_iota(jnp.int32, (bands * ROWS, count), 0) % ROWS
    digits = jnp.where(row == CH, source // BLOCK, 0)
    digits = jnp.where(row == CH + 1, source % BLOCK, digits)
    digits = jnp.where(row == CH + 2, receiver // 256, digits)
    digits = jnp.where(row == CH + 3, receiver % 256, digits)
    spectra = contract_last(twiddle_ref[...], traces_ref[0])
    packed = (spectra + digits.astype(jnp.float32)).astype(jnp.bfloat16)
    ordered = contract_last(packed, permute)
    for band in range(bands):
        part = ordered[band * ROWS : (band + 1) * ROWS].astype(jnp.bfloat16)
        for tile in range(tiles):
            out_ref[band, tile] = part


def merge_group(first_run, lists_ref, flat, packed, keys, counts, counts_s, chunks_s, sem):
    length = lists_ref.shape[2]

    for r in range(GROUP):
        part = lists_ref[first_run + r].astype(jnp.float32)
        keys[r : r + 1, :] = part[CH : CH + 1]
        for first in range(0, length, 128):
            at = r * length + first
            flat[at : at + 128, :ROWS] = jnp.transpose(part[:, first : first + 128])

    block_of = keys[...]
    lane = lax.broadcasted_iota(jnp.int32, (GROUP, 128), 1)
    starts = jnp.zeros((GROUP, 128), jnp.float32)
    for b in range(1, BLOCKS + 1):
        below = jnp.sum((block_of < float(b)).astype(jnp.float32), axis=1, keepdims=True)
        starts = jnp.where(lane == b, below, starts)
    starts = starts.astype(jnp.int32)
    widest = jnp.max(pltpu.roll(starts, 127, 1) - starts, axis=0, keepdims=True)
    counts[:GROUP, :] = starts
    counts[GROUP:, :] = jnp.broadcast_to(widest, (8, 128))
    copy = pltpu.make_async_copy(counts, counts_s, sem)
    copy.start()
    copy.wait()

    def block(b, carry):
        base, filled = carry

        def plain():
            at = base
            for r in range(GROUP):
                start = counts_s[r, b]
                packed[pl.ds(at, COPY), :] = flat[pl.ds(r * length + start, COPY), :]
                at = at + (counts_s[r, b + 1] - start)
            return at

        def long():
            def run(r, at):
                start = counts_s[r, b]
                size = counts_s[r, b + 1] - start

                def piece(k, _):
                    packed[pl.ds(at + 8 * k, 8), :] = flat[pl.ds(r * length + start + 8 * k, 8), :]
                    return 0

                lax.fori_loop(0, (size + 7) // 8, piece, 0)
                return at + size

            return lax.fori_loop(0, GROUP, run, base)

        end = lax.cond(counts_s[GROUP, b] <= COPY, plain, long)
        size = end - base

        def entry(k, at):
            chunks_s[0, at] = b
            chunks_s[1, at] = base + k * CHUNK
            chunks_s[2, at] = size - k * CHUNK
            return at + 1

        filled = lax.fori_loop(0, (size + CHUNK - 1) // CHUNK, entry, filled)
        return (end + 7) // 8 * 8, filled

    _, filled = lax.fori_loop(0, BLOCKS, block, (jnp.int32(0), jnp.int32(0)))
    padded = (filled + UNROLL - 1) // UNROLL * UNROLL

    def pad(at, _):
        chunks_s[0, at] = 0
        chunks_s[1, at] = 0
        chunks_s[2, at] = 0
        return 0

    lax.fori_loop(filled, padded, pad, 0)
    return padded


def add_chunks(chunk_count, packed, chunks_s, grid):
    row = lax.broadcasted_iota(jnp.int32, (BLOCK, CHUNK), 0).astype(jnp.float32)
    place = lax.broadcasted_iota(jnp.int32, (BLOCK, CHUNK), 1)
    column = lax.broadcasted_iota(jnp.int32, (NG, CHUNK), 0).astype(jnp.float32)

    def product(i):
        first = pl.multiple_of(chunks_s[1, i], 8)
        part = jnp.concatenate(
            [
                jnp.transpose(packed[pl.ds(first + k, 128), :])[:ROWS]
                for k in range(0, CHUNK, 128)
            ],
            axis=1,
        )
        hit = (part[CH + 1 : CH + 2] == row) & (place < chunks_s[2, i])
        left = [jnp.where(hit, part[c : c + 1], 0.0).astype(jnp.bfloat16) for c in range(CH)]
        left.append(jnp.where(hit, 1.0, 0.0).astype(jnp.bfloat16))
        receiver = part[CH + 2 : CH + 3] * 256.0 + part[CH + 3 : CH + 4]
        right = jnp.where(receiver == column, 1.0, 0.0).astype(jnp.bfloat16)
        return contract_last(jnp.concatenate(left, axis=0), right)

    def body(step, _):
        products = [product(step * UNROLL + q) for q in range(UNROLL)]
        for q in range(UNROLL):
            rows = pl.ds(pl.multiple_of(chunks_s[0, step * UNROLL + q] * BLOCK, BLOCK), BLOCK)
            for c in range(CH + 1):
                grid[c, rows, :] += products[q][c * BLOCK : (c + 1) * BLOCK]
        return 0

    lax.fori_loop(0, chunk_count // UNROLL, body, 0)


def grid_kernel(
    scale, row_block, lists_ref, out_ref, grid, planes, flat, packed, keys, counts, turned,
    counts_s, chunks_s, sem
):
    runs = lists_ref.shape[0]
    grid[...] = jnp.zeros_like(grid)

    def group(g):
        chunk_count = merge_group(
            g * GROUP, lists_ref, flat, packed, keys, counts, counts_s, chunks_s, sem
        )
        add_chunks(chunk_count, packed, chunks_s, grid)

    if runs == GROUP:
        group(0)
    else:
        lax.fori_loop(0, runs // GROUP, lambda g, _: (group(g), 0)[1], 0)

    grid[CH] = 1.0 / jnp.maximum(grid[CH], 1.0)

    first_row = pl.multiple_of(lax.axis_index("tile") * row_block, row_block)
    first_col = pl.multiple_of(first_row // 128 * 128, 128)
    within = pl.multiple_of(first_row % 128, row_block)

    def own_rows(p):
        turned[...] = jnp.transpose(planes[p, :, pl.ds(first_col, 128)].astype(jnp.float32))
        across = turned[pl.ds(within, row_block), :]
        along = planes[p, pl.ds(first_row, row_block), :].astype(jnp.float32)
        return (0.5 * (along + across)).astype(jnp.bfloat16)

    def frequency(f, _):
        planes[0] = (grid[f] * grid[CH]).astype(jnp.bfloat16)
        planes[1] = (grid[FB + f] * grid[CH]).astype(jnp.bfloat16)
        own = jnp.concatenate([own_rows(0), own_rows(1)], axis=0)
        real = planes[0]
        imag = planes[1]
        by_real = jnp.dot(own, real, preferred_element_type=jnp.float32) + contract_last(own, real)
        by_imag = jnp.dot(own, imag, preferred_element_type=jnp.float32) + contract_last(own, imag)
        half = 0.5 * scale
        out_ref[f, 0] = (by_real[:row_block] - by_imag[row_block:]) * half
        out_ref[f, 1] = (by_imag[:row_block] + by_real[row_block:]) * half
        return 0

    lax.fori_loop(0, FB, frequency, 0)


def whole(space=pltpu.VMEM):
    return pl.BlockSpec(memory_space=space)


def per_device(raw_traces, bin_owner, bin_offset):
    band_count = lax.axis_size("band")
    tile_count = lax.axis_size("tile")
    length = bin_offset.shape[1]
    count = raw_traces.shape[1]
    cells_dev = NG * NG // tile_count
    row_block = NG // tile_count
    runs = band_count * tile_count
    params = pltpu.CompilerParams(vmem_limit_bytes=VMEM)

    own = pl.pallas_call(
        functools.partial(run_kernel, cells_dev),
        out_shape=jax.ShapeDtypeStruct((band_count, tile_count, ROWS, count), jnp.bfloat16),
        in_specs=[whole()] * 4,
        out_specs=whole(),
        compiler_params=params,
        name="own_run",
    )(
        jnp.asarray(twiddle_rows(band_count)),
        raw_traces,
        bin_owner.reshape(1, length),
        bin_offset,
    )
    lists = lax.all_to_all(
        own.reshape(runs, ROWS, count), ("band", "tile"), split_axis=0, concat_axis=0, tiled=True
    )

    traces = GROUP * count
    slots = traces + BLOCKS * 8 + CHUNK + COPY
    return pl.pallas_call(
        functools.partial(grid_kernel, 1.0 / math.sqrt(NG), row_block),
        out_shape=jax.ShapeDtypeStruct((FB, 2, row_block, NG), jnp.float32),
        in_specs=[whole()],
        out_specs=whole(),
        scratch_shapes=[
            pltpu.VMEM((CH + 1, NG, NG), jnp.float32),
            pltpu.VMEM((2, NG, NG), jnp.bfloat16),
            pltpu.VMEM((traces + COPY, 128), jnp.float32),
            pltpu.VMEM((slots, 128), jnp.float32),
            pltpu.VMEM((GROUP, count), jnp.float32),
            pltpu.VMEM((GROUP + 8, 128), jnp.int32),
            pltpu.VMEM((128, NG), jnp.float32),
            pltpu.SMEM((GROUP + 8, 128), jnp.int32),
            pltpu.SMEM((3, traces // CHUNK + BLOCKS + UNROLL), jnp.int32),
            pltpu.SemaphoreType.DMA,
        ],
        compiler_params=params,
        name="grid",
    )(lists)


def solution(mesh):
    return jax.shard_map(
        per_device,
        mesh=mesh,
        in_specs=(P("tile", "band", None), P("tile", None, None), P("tile", None)),
        out_specs=P("band", None, "tile", None),
        check_vma=False,
    )
```

time: 324 us -> 54 us (0.17)
  waiting for transfers between devices: 159 us -> 0 us
  local copies, waits for them, and re-layouts: 65.4 us -> 0 us
  other arithmetic: 62.5 us -> 0 us
  Pallas kernels: 0 us -> 33 us
  blocking collectives: 0 us -> 21 us
  starting transfers between devices: 14 us -> 0 us
  between operations: 13.6 us -> 0.01 us
  matrix products: 7.21 us -> 0 us
    all_gather x1 -> x0, waiting for transfers between devices: 149 us -> none  [per_device(): gathered = lax.all_gather(grid_field, 'tile', axis=2, tiled=True)]
    scatter-add x2 -> x0, other arithmetic: 33.1 us -> none  [the longest x1 19.9 us: per_device(): jax.ops.segment_sum(slot_values, arrived_cells, cells_dev + 1)[:cells_dev]]
    pallas_call x0 -> x2, Pallas kernels: none -> 33 us  [the longest x1 30.3 us: per_device(): pl.pallas_call(functools.partial(grid_kernel, 1.0 / math.sqrt(NG), row_bl...]
    all_gather x1 -> x0, local copies, waits for them, and re-layouts: 26 us -> none  [per_device(): gathered = lax.all_gather(grid_field, 'tile', axis=2, tiled=True)]
    all_to_all x0 -> x1, blocking collectives: none -> 21 us  [per_device(): lax.all_to_all(own.reshape(runs, ROWS, count), ('band', 'tile'), split_ax...]
    convert_element_type x3 -> x0, local copies, waits for them, and re-layouts: 16.8 us -> none  [the longest x1 16.3 us: per_device(): gathered.astype(jnp.float32)]
    all_to_all x3 -> x0, starting transfers between devices: 13.9 us -> none  [the longest x1 7.28 us: per_device(): lax.all_to_all(labels, 'tile', split_axis=0, concat_axis=0, tiled=True)]
    convert_element_type x3 -> x0, other arithmetic: 12 us -> none  [the longest x1 11.2 us: per_device(): symmetric_all = (0.5 * (gathered.astype(jnp.float32) + jnp.swapaxes(gathe...]
  transfers between devices with their start and end apart: 4 -> 0, of which waited for: 3 -> 0; matrix products, arithmetic and copies ran while one was open for 5% -> 0% of each run, Pallas kernels for 0% -> 0%
where the time goes in v2:
time: 54 us
  Pallas kernels  33 us (61%)
  blocking collectives  21 us (39%)
    pallas_call x1, Pallas kernels, per_device(): pl.pallas_call(functools.partial(grid_kernel, 1.0 / math.sqrt(NG), row_bl...  30.3 us
    all_to_all x1, blocking collectives, per_device(): lax.all_to_all(own.reshape(runs, ROWS, count), ('band', 'tile'), split_ax...  21 us
    pallas_call x1, Pallas kernels, per_device(): pl.pallas_call(functools.partial(run_kernel, cells_dev), out_shape=jax.Sh...  2.71 us

profile of v2, /device:TPU:0, one launch (start us, length us, event | category | flops | bytes accessed | tf_op | source)
XLA Modules:
  0.0 54.0 jit_solution(11537936382838747315)
XLA Ops:
  0.0 2.7 %own_run.1 = bf16[4,8,24,256]{3,2,1,0:T(8,128)(2,1)} custom-call(bf16[96,2048]{1,0:T(8,128)(2,1)} %constant.2.clone.twiddle_ref, bf16[1,256,2048]{2,1,0:T(8,128)(2,1)} %traces_ref.1, s32[1,1024]{1,0:T(1,128)} %bitcast.3, s32[1,1024]{1,0:T(1,128)} %offset_ref.1), custom_call_target="tpu_custom_call" | custom-call | tf_op jit(solution)/shard_map/own_run/pallas_call | solution.py:238
  2.7 21.0 %all_to_all.5.lists_ref = bf16[32,24,256]{2,1,0:T(8,128)(2,1)} all-to-all(bf16[32,24,256]{2,1,0:T(8,128)(2,1)} %bitcast.2), channel_id=1, replica_groups=mesh['band'=4,'tile'=8] {'band','tile'}, dimensions={0} | all-to-all | bytes 786432 | tf_op jit(solution)/shard_map/all_to_all | solution.py:251
  23.7 30.3 %grid.1 = f32[10,2,64,512]{3,2,1,0:T(8,128)} custom-call(bf16[32,24,256]{2,1,0:T(8,128)(2,1)} %all_to_all.5.lists_ref), custom_call_target="tpu_custom_call" | custom-call | tf_op jit(solution)/shard_map/grid/pallas_call | solution.py:257

commit v3 on v2

--- a/solution.py
+++ b/solution.py
@@ -19,7 +19,8 @@
 BLOCKS = NG // BLOCK
 GROUP = 32
 COPY = 32
-CHUNK = 256
+SMALL = 256
+LARGE = 512
 UNROLL = 2
 VMEM = 56 * 1024 * 1024
 
@@ -69,16 +70,11 @@
             out_ref[band, tile] = part
 
 
-def merge_group(first_run, lists_ref, flat, packed, keys, counts, counts_s, chunks_s, sem):
+def merge_group(first_run, lists_ref, flat, packed, keys, counts, counts_s, lists_s, sem, alone):
     length = lists_ref.shape[2]
 
     for r in range(GROUP):
-        part = lists_ref[first_run + r].astype(jnp.float32)
-        keys[r : r + 1, :] = part[CH : CH + 1]
-        for first in range(0, length, 128):
-            at = r * length + first
-            flat[at : at + 128, :ROWS] = jnp.transpose(part[:, first : first + 128])
-
+        keys[r : r + 1, :] = lists_ref[first_run + r].astype(jnp.float32)[CH : CH + 1]
     block_of = keys[...]
     lane = lax.broadcasted_iota(jnp.int32, (GROUP, 128), 1)
     starts = jnp.zeros((GROUP, 128), jnp.float32)
@@ -91,10 +87,15 @@
     counts[GROUP:, :] = jnp.broadcast_to(widest, (8, 128))
     copy = pltpu.make_async_copy(counts, counts_s, sem)
     copy.start()
+    for r in range(GROUP):
+        part = lists_ref[first_run + r].astype(jnp.float32)
+        for first in range(0, length, 128):
+            at = r * length + first
+            flat[at : at + 128, :ROWS] = jnp.transpose(part[:, first : first + 128])
     copy.wait()
 
     def block(b, carry):
-        base, filled = carry
+        base, filled = carry[0], list(carry[1:])
 
         def plain():
             at = base
@@ -120,105 +121,157 @@
 
         end = lax.cond(counts_s[GROUP, b] <= COPY, plain, long)
         size = end - base
-
-        def entry(k, at):
-            chunks_s[0, at] = b
-            chunks_s[1, at] = base + k * CHUNK
-            chunks_s[2, at] = size - k * CHUNK
-            return at + 1
-
-        filled = lax.fori_loop(0, (size + CHUNK - 1) // CHUNK, entry, filled)
-        return (end + 7) // 8 * 8, filled
-
-    _, filled = lax.fori_loop(0, BLOCKS, block, (jnp.int32(0), jnp.int32(0)))
-    padded = (filled + UNROLL - 1) // UNROLL * UNROLL
-
-    def pad(at, _):
-        chunks_s[0, at] = 0
-        chunks_s[1, at] = 0
-        chunks_s[2, at] = 0
+        kind = (size > SMALL).astype(jnp.int32) + (size > LARGE).astype(jnp.int32)
+        at = jnp.where(kind == 0, filled[0], jnp.where(kind == 1, filled[1], filled[2]))
+        lists_s[3 * kind, at] = b
+        lists_s[3 * kind + 1, at] = base
+        lists_s[3 * kind + 2, at] = size
+        filled = [filled[k] + (kind == k).astype(jnp.int32) for k in range(3)]
+        return ((end + 7) // 8 * 8, *filled)
+
+    zero = jnp.int32(0)
+    _, *filled = lax.fori_loop(0, BLOCKS, block, (zero,) * 4)
+    for kind in range(2):
+
+        def pad(at, _, kind=kind):
+            last = at - 1
+            lists_s[3 * kind, at] = lists_s[3 * kind, last]
+            lists_s[3 * kind + 1, at] = lists_s[3 * kind + 1, last]
+            lists_s[3 * kind + 2, at] = lists_s[3 * kind + 2, last] if alone else 0
+            return 0
+
+        whole_steps = (filled[kind] + UNROLL - 1) // UNROLL * UNROLL
+        lax.fori_loop(filled[kind], whole_steps, pad, 0)
+        filled[kind] = whole_steps
+    return filled
+
+
+def product(first, size, width, packed):
+    part = jnp.concatenate(
+        [jnp.transpose(packed[pl.ds(first + k, 128), :])[:ROWS] for k in range(0, width, 128)],
+        axis=1,
+    )
+    step = lax.broadcasted_iota(jnp.int32, (BLOCK, width), 0).astype(jnp.float32)
+    step = step.astype(jnp.bfloat16)
+    place = lax.broadcasted_iota(jnp.int32, (1, width), 1)
+    one = jnp.ones((), jnp.bfloat16)
+    none = jnp.zeros((), jnp.bfloat16)
+
+    def spread(row):
+        return jnp.broadcast_to(row, (BLOCK, width)).astype(jnp.bfloat16)
+
+    hit = spread(jnp.where(place < size, part[CH + 1 : CH + 2], -1.0)) == step
+    left = [jnp.where(hit, spread(part[c : c + 1]), none) for c in range(CH)]
+    left.append(jnp.where(hit, one, none))
+    right = []
+    for half in range(NG // 256):
+        low = spread(jnp.where(part[CH + 2 : CH + 3] == float(half), part[CH + 3 : CH + 4], -1.0))
+        for j in range(0, 256, BLOCK):
+            right.append(jnp.where(low == step + jnp.bfloat16(j), one, none))
+    return contract_last(jnp.concatenate(left, axis=0), jnp.concatenate(right, axis=0))
+
+
+def block_rows(b):
+    return pl.ds(pl.multiple_of(b * BLOCK, BLOCK), BLOCK)
+
+
+def add_blocks(filled, packed, lists_s, total, emit):
+    for kind, width in ((0, SMALL), (1, LARGE)):
+
+        def body(step, _, kind=kind, width=width):
+            sums = []
+            for q in range(UNROLL):
+                at = step * UNROLL + q
+                first = pl.multiple_of(lists_s[3 * kind + 1, at], 8)
+                sums.append(product(first, lists_s[3 * kind + 2, at], width, packed))
+            for q in range(UNROLL):
+                emit(lists_s[3 * kind, step * UNROLL + q], sums[q])
+            return 0
+
+        lax.fori_loop(0, filled[kind] // UNROLL, body, 0)
+
+    def long(at, _):
+        total[...] = jnp.zeros_like(total)
+        size = lists_s[8, at]
+
+        def piece(k, _):
+            first = pl.multiple_of(lists_s[7, at] + k * LARGE, 8)
+            total[...] += product(first, size - k * LARGE, LARGE, packed)
+            return 0
+
+        lax.fori_loop(0, (size + LARGE - 1) // LARGE, piece, 0)
+        emit(lists_s[6, at], total[...])
         return 0
 
-    lax.fori_loop(filled, padded, pad, 0)
-    return padded
-
-
-def add_chunks(chunk_count, packed, chunks_s, grid):
-    row = lax.broadcasted_iota(jnp.int32, (BLOCK, CHUNK), 0).astype(jnp.float32)
-    place = lax.broadcasted_iota(jnp.int32, (BLOCK, CHUNK), 1)
-    column = lax.broadcasted_iota(jnp.int32, (NG, CHUNK), 0).astype(jnp.float32)
-
-    def product(i):
-        first = pl.multiple_of(chunks_s[1, i], 8)
-        part = jnp.concatenate(
-            [
-                jnp.transpose(packed[pl.ds(first + k, 128), :])[:ROWS]
-                for k in range(0, CHUNK, 128)
-            ],
-            axis=1,
-        )
-        hit = (part[CH + 1 : CH + 2] == row) & (place < chunks_s[2, i])
-        left = [jnp.where(hit, part[c : c + 1], 0.0).astype(jnp.bfloat16) for c in range(CH)]
-        left.append(jnp.where(hit, 1.0, 0.0).astype(jnp.bfloat16))
-        receiver = part[CH + 2 : CH + 3] * 256.0 + part[CH + 3 : CH + 4]
-        right = jnp.where(receiver == column, 1.0, 0.0).astype(jnp.bfloat16)
-        return contract_last(jnp.concatenate(left, axis=0), right)
-
-    def body(step, _):
-        products = [product(step * UNROLL + q) for q in range(UNROLL)]
-        for q in range(UNROLL):
-            rows = pl.ds(pl.multiple_of(chunks_s[0, step * UNROLL + q] * BLOCK, BLOCK), BLOCK)
-            for c in range(CH + 1):
-                grid[c, rows, :] += products[q][c * BLOCK : (c + 1) * BLOCK]
-        return 0
-
-    lax.fori_loop(0, chunk_count // UNROLL, body, 0)
+    lax.fori_loop(0, filled[2], long, 0)
 
 
 def grid_kernel(
-    scale, row_block, lists_ref, out_ref, grid, planes, flat, packed, keys, counts, turned,
-    counts_s, chunks_s, sem
+    scale, row_block, lists_ref, out_ref, planes, flat, packed, keys, counts, turned, total,
+    counts_s, lists_s, sem, grid=None
 ):
     runs = lists_ref.shape[0]
-    grid[...] = jnp.zeros_like(grid)
-
-    def group(g):
-        chunk_count = merge_group(
-            g * GROUP, lists_ref, flat, packed, keys, counts, counts_s, chunks_s, sem
+    alone = runs == GROUP
+
+    def finish(sums, inverse, rows):
+        for c in range(CH):
+            planes[c, rows, :] = (sums(c) * inverse).astype(jnp.bfloat16)
+
+    def emit(b, sums):
+        rows = block_rows(b)
+        if alone:
+            inverse = 1.0 / jnp.maximum(sums[CH * BLOCK :], 1.0)
+            finish(lambda c: sums[c * BLOCK : (c + 1) * BLOCK], inverse, rows)
+        else:
+            for c in range(CH + 1):
+                grid[c, rows, :] += sums[c * BLOCK : (c + 1) * BLOCK]
+
+    def group(g, _):
+        filled = merge_group(
+            g * GROUP, lists_ref, flat, packed, keys, counts, counts_s, lists_s, sem, alone
         )
-        add_chunks(chunk_count, packed, chunks_s, grid)
-
-    if runs == GROUP:
-        group(0)
+        add_blocks(filled, packed, lists_s, total, emit)
+        return 0
+
+    if alone:
+        group(0, 0)
     else:
-        lax.fori_loop(0, runs // GROUP, lambda g, _: (group(g), 0)[1], 0)
-
-    grid[CH] = 1.0 / jnp.maximum(grid[CH], 1.0)
+        grid[...] = jnp.zeros_like(grid)
+        lax.fori_loop(0, runs // GROUP, group, 0)
+
+        def divide(b, _):
+            rows = block_rows(b)
+            finish(lambda c: grid[c, rows, :], 1.0 / jnp.maximum(grid[CH, rows, :], 1.0), rows)
+            return 0
+
+        lax.fori_loop(0, BLOCKS, divide, 0)
 
     first_row = pl.multiple_of(lax.axis_index("tile") * row_block, row_block)
     first_col = pl.multiple_of(first_row // 128 * 128, 128)
     within = pl.multiple_of(first_row % 128, row_block)
 
-    def own_rows(p):
-        turned[...] = jnp.transpose(planes[p, :, pl.ds(first_col, 128)].astype(jnp.float32))
-        across = turned[pl.ds(within, row_block), :]
+    def own_rows(p, slot):
+        turned[slot] = jnp.transpose(planes[p, :, pl.ds(first_col, 128)].astype(jnp.float32))
+        across = turned[slot, pl.ds(within, row_block), :]
         along = planes[p, pl.ds(first_row, row_block), :].astype(jnp.float32)
         return (0.5 * (along + across)).astype(jnp.bfloat16)
 
-    def frequency(f, _):
-        planes[0] = (grid[f] * grid[CH]).astype(jnp.bfloat16)
-        planes[1] = (grid[FB + f] * grid[CH]).astype(jnp.bfloat16)
-        own = jnp.concatenate([own_rows(0), own_rows(1)], axis=0)
-        real = planes[0]
-        imag = planes[1]
+    def frequency(f, slot):
+        own = jnp.concatenate([own_rows(f, slot), own_rows(FB + f, slot + 1)], axis=0)
+        real = planes[f]
+        imag = planes[FB + f]
         by_real = jnp.dot(own, real, preferred_element_type=jnp.float32) + contract_last(own, real)
         by_imag = jnp.dot(own, imag, preferred_element_type=jnp.float32) + contract_last(own, imag)
         half = 0.5 * scale
         out_ref[f, 0] = (by_real[:row_block] - by_imag[row_block:]) * half
         out_ref[f, 1] = (by_imag[:row_block] + by_real[row_block:]) * half
+
+    def pair(i, _):
+        frequency(2 * i, 0)
+        frequency(2 * i + 1, 2)
         return 0
 
-    lax.fori_loop(0, FB, frequency, 0)
+    lax.fori_loop(0, FB // 2, pair, 0)
 
 
 def whole(space=pltpu.VMEM):
@@ -253,24 +306,27 @@
     )
 
     traces = GROUP * count
-    slots = traces + BLOCKS * 8 + CHUNK + COPY
+    slots = traces + BLOCKS * 8 + LARGE + COPY
+    scratch = [
+        pltpu.VMEM((CH, NG, NG), jnp.bfloat16),
+        pltpu.VMEM((traces + COPY, 128), jnp.float32),
+        pltpu.VMEM((slots, 128), jnp.float32),
+        pltpu.VMEM((GROUP, count), jnp.float32),
+        pltpu.VMEM((GROUP + 8, 128), jnp.int32),
+        pltpu.VMEM((4, 128, NG), jnp.float32),
+        pltpu.VMEM(((CH + 1) * BLOCK, NG), jnp.float32),
+        pltpu.SMEM((GROUP + 8, 128), jnp.int32),
+        pltpu.SMEM((9, BLOCKS + UNROLL), jnp.int32),
+        pltpu.SemaphoreType.DMA,
+    ]
+    if runs != GROUP:
+        scratch.append(pltpu.VMEM((CH + 1, NG, NG), jnp.float32))
     return pl.pallas_call(
         functools.partial(grid_kernel, 1.0 / math.sqrt(NG), row_block),
         out_shape=jax.ShapeDtypeStruct((FB, 2, row_block, NG), jnp.float32),
         in_specs=[whole()],
         out_specs=whole(),
-        scratch_shapes=[
-            pltpu.VMEM((CH + 1, NG, NG), jnp.float32),
-            pltpu.VMEM((2, NG, NG), jnp.bfloat16),
-            pltpu.VMEM((traces + COPY, 128), jnp.float32),
-            pltpu.VMEM((slots, 128), jnp.float32),
-            pltpu.VMEM((GROUP, count), jnp.float32),
-            pltpu.VMEM((GROUP + 8, 128), jnp.int32),
-            pltpu.VMEM((128, NG), jnp.float32),
-            pltpu.SMEM((GROUP + 8, 128), jnp.int32),
-            pltpu.SMEM((3, traces // CHUNK + BLOCKS + UNROLL), jnp.int32),
-            pltpu.SemaphoreType.DMA,
-        ],
+        scratch_shapes=scratch,
         compiler_params=params,
         name="grid",
     )(lists)

time: 54 us -> 49 us (0.907)
  Pallas kernels: 33 us -> 27.8 us
    pallas_call x1, Pallas kernels: 30.3 us -> 25.1 us  [per_device(): pl.pallas_call(functools.partial(grid_kernel, 1.0 / math.sqrt(NG), row_bl...]
where the time goes in v3:
time: 49 us; the launch traced here: 48.7 us
  Pallas kernels  27.8 us (57%)
  blocking collectives  21 us (43%)
    pallas_call x1, Pallas kernels, per_device(): pl.pallas_call(functools.partial(grid_kernel, 1.0 / math.sqrt(NG), row_bl...  25.1 us
    all_to_all x1, blocking collectives, per_device(): lax.all_to_all(own.reshape(runs, ROWS, count), ('band', 'tile'), split_ax...  21 us
    pallas_call x1, Pallas kernels, per_device(): pl.pallas_call(functools.partial(run_kernel, cells_dev), out_shape=jax.Sh...  2.71 us

profile of v3, /device:TPU:0, one launch (start us, length us, event | category | flops | bytes accessed | tf_op | source)
XLA Modules:
  0.0 48.7 jit_solution(17318770582617862239)
XLA Ops:
  0.0 2.7 %own_run.1 = bf16[4,8,24,256]{3,2,1,0:T(8,128)(2,1)} custom-call(bf16[96,2048]{1,0:T(8,128)(2,1)} %constant.2.clone.twiddle_ref, bf16[1,256,2048]{2,1,0:T(8,128)(2,1)} %traces_ref.1, s32[1,1024]{1,0:T(1,128)} %bitcast.3, s32[1,1024]{1,0:T(1,128)} %offset_ref.1), custom_call_target="tpu_custom_call" | custom-call | tf_op jit(solution)/shard_map/own_run/pallas_call | solution.py:291
  2.7 21.0 %all_to_all.5.lists_ref = bf16[32,24,256]{2,1,0:T(8,128)(2,1)} all-to-all(bf16[32,24,256]{2,1,0:T(8,128)(2,1)} %bitcast.2), channel_id=1, replica_groups=mesh['band'=4,'tile'=8] {'band','tile'}, dimensions={0} | all-to-all | bytes 786432 | tf_op jit(solution)/shard_map/all_to_all | solution.py:304
  23.7 25.1 %grid.1 = f32[10,2,64,512]{3,2,1,0:T(8,128)} custom-call(bf16[32,24,256]{2,1,0:T(8,128)(2,1)} %all_to_all.5.lists_ref), custom_call_target="tpu_custom_call" | custom-call | tf_op jit(solution)/shard_map/grid/pallas_call | solution.py:324

commit v4 on v3

--- a/solution.py
+++ b/solution.py
@@ -21,7 +21,7 @@
 COPY = 32
 SMALL = 256
 LARGE = 512
-UNROLL = 2
+SIDE = 4
 VMEM = 56 * 1024 * 1024
 
 
@@ -70,9 +70,8 @@
             out_ref[band, tile] = part
 
 
-def merge_group(first_run, lists_ref, flat, packed, keys, counts, counts_s, lists_s, sem, alone):
+def make_table(first_run, lists_ref, keys, table, table_s, sem):
     length = lists_ref.shape[2]
-
     for r in range(GROUP):
         keys[r : r + 1, :] = lists_ref[first_run + r].astype(jnp.float32)[CH : CH + 1]
     block_of = keys[...]
@@ -81,69 +80,34 @@
     for b in range(1, BLOCKS + 1):
         below = jnp.sum((block_of < float(b)).astype(jnp.float32), axis=1, keepdims=True)
         starts = jnp.where(lane == b, below, starts)
-    starts = starts.astype(jnp.int32)
-    widest = jnp.max(pltpu.roll(starts, 127, 1) - starts, axis=0, keepdims=True)
-    counts[:GROUP, :] = starts
-    counts[GROUP:, :] = jnp.broadcast_to(widest, (8, 128))
-    copy = pltpu.make_async_copy(counts, counts_s, sem)
+    sizes = jnp.where(lane < BLOCKS, pltpu.roll(starts, 127, 1) - starts, 0.0)
+    earlier = lax.broadcasted_iota(jnp.int32, (GROUP, GROUP), 0) > lax.broadcasted_iota(
+        jnp.int32, (GROUP, GROUP), 1
+    )
+    targets = jnp.dot(
+        earlier.astype(jnp.float32).astype(jnp.bfloat16),
+        sizes.astype(jnp.bfloat16),
+        preferred_element_type=jnp.float32,
+    )
+    run = lax.broadcasted_iota(jnp.int32, (GROUP, 128), 0)
+    table[:GROUP, :] = starts.astype(jnp.int32) + run * length
+    table[GROUP : 2 * GROUP, :] = targets.astype(jnp.int32)
+    widest = jnp.max(sizes, axis=0, keepdims=True)
+    total = jnp.sum(sizes, axis=0, keepdims=True)
+    last = lax.broadcasted_iota(jnp.int32, (8, 128), 0)
+    table[2 * GROUP :, :] = jnp.where(last == 0, widest, total).astype(jnp.int32)
+    copy = pltpu.make_async_copy(table, table_s, sem)
     copy.start()
+    return copy
+
+
+def turn_runs(first_run, lists_ref, flat):
+    length = lists_ref.shape[2]
     for r in range(GROUP):
         part = lists_ref[first_run + r].astype(jnp.float32)
         for first in range(0, length, 128):
             at = r * length + first
             flat[at : at + 128, :ROWS] = jnp.transpose(part[:, first : first + 128])
-    copy.wait()
-
-    def block(b, carry):
-        base, filled = carry[0], list(carry[1:])
-
-        def plain():
-            at = base
-            for r in range(GROUP):
-                start = counts_s[r, b]
-                packed[pl.ds(at, COPY), :] = flat[pl.ds(r * length + start, COPY), :]
-                at = at + (counts_s[r, b + 1] - start)
-            return at
-
-        def long():
-            def run(r, at):
-                start = counts_s[r, b]
-                size = counts_s[r, b + 1] - start
-
-                def piece(k, _):
-                    packed[pl.ds(at + 8 * k, 8), :] = flat[pl.ds(r * length + start + 8 * k, 8), :]
-                    return 0
-
-                lax.fori_loop(0, (size + 7) // 8, piece, 0)
-                return at + size
-
-            return lax.fori_loop(0, GROUP, run, base)
-
-        end = lax.cond(counts_s[GROUP, b] <= COPY, plain, long)
-        size = end - base
-        kind = (size > SMALL).astype(jnp.int32) + (size > LARGE).astype(jnp.int32)
-        at = jnp.where(kind == 0, filled[0], jnp.where(kind == 1, filled[1], filled[2]))
-        lists_s[3 * kind, at] = b
-        lists_s[3 * kind + 1, at] = base
-        lists_s[3 * kind + 2, at] = size
-        filled = [filled[k] + (kind == k).astype(jnp.int32) for k in range(3)]
-        return ((end + 7) // 8 * 8, *filled)
-
-    zero = jnp.int32(0)
-    _, *filled = lax.fori_loop(0, BLOCKS, block, (zero,) * 4)
-    for kind in range(2):
-
-        def pad(at, _, kind=kind):
-            last = at - 1
-            lists_s[3 * kind, at] = lists_s[3 * kind, last]
-            lists_s[3 * kind + 1, at] = lists_s[3 * kind + 1, last]
-            lists_s[3 * kind + 2, at] = lists_s[3 * kind + 2, last] if alone else 0
-            return 0
-
-        whole_steps = (filled[kind] + UNROLL - 1) // UNROLL * UNROLL
-        lax.fori_loop(filled[kind], whole_steps, pad, 0)
-        filled[kind] = whole_steps
-    return filled
 
 
 def product(first, size, width, packed):
@@ -175,43 +139,78 @@
     return pl.ds(pl.multiple_of(b * BLOCK, BLOCK), BLOCK)
 
 
-def add_blocks(filled, packed, lists_s, total, emit):
-    for kind, width in ((0, SMALL), (1, LARGE)):
-
-        def body(step, _, kind=kind, width=width):
-            sums = []
-            for q in range(UNROLL):
-                at = step * UNROLL + q
-                first = pl.multiple_of(lists_s[3 * kind + 1, at], 8)
-                sums.append(product(first, lists_s[3 * kind + 2, at], width, packed))
-            for q in range(UNROLL):
-                emit(lists_s[3 * kind, step * UNROLL + q], sums[q])
+def add_blocks(table_s, flat, buffers, packed, total, emit):
+    def fast(b, width):
+        sums = []
+        for q in range(SIDE):
+            buffer = buffers[q]
+            for r in range(GROUP):
+                buffer[pl.ds(table_s[GROUP + r, b + q], COPY), :] = flat[
+                    pl.ds(table_s[r, b + q], COPY), :
+                ]
+            sums.append(product(0, table_s[2 * GROUP + 1, b + q], width, buffer))
+        for q in range(SIDE):
+            emit(b + q, sums[q])
+
+    def slow(b):
+        def run(r, _):
+            source = table_s[r, b]
+            target = table_s[GROUP + r, b]
+            after = table_s[2 * GROUP + 1, b]
+            after = jnp.where(r + 1 < GROUP, table_s[jnp.minimum(GROUP + r + 1, 2 * GROUP - 1), b], after)
+
+            def piece(k, _):
+                packed[pl.ds(target + 8 * k, 8), :] = flat[pl.ds(source + 8 * k, 8), :]
+                return 0
+
+            return lax.fori_loop(0, (after - target + 7) // 8, piece, 0)
+
+        lax.fori_loop(0, GROUP, run, 0)
+        total[...] = jnp.zeros_like(total)
+        size = table_s[2 * GROUP + 1, b]
+
+        def piece(k, _):
+            first = pl.multiple_of(k * LARGE, LARGE)
+            total[...] += product(first, size - first, LARGE, packed)
             return 0
 
-        lax.fori_loop(0, filled[kind] // UNROLL, body, 0)
-
-    def long(at, _):
-        total[...] = jnp.zeros_like(total)
-        size = lists_s[8, at]
-
-        def piece(k, _):
-            first = pl.multiple_of(lists_s[7, at] + k * LARGE, 8)
-            total[...] += product(first, size - k * LARGE, LARGE, packed)
-            return 0
-
         lax.fori_loop(0, (size + LARGE - 1) // LARGE, piece, 0)
-        emit(lists_s[6, at], total[...])
+        emit(b, total[...])
+
+    def side(i, _):
+        b = i * SIDE
+        widest = table_s[2 * GROUP, b]
+        largest = table_s[2 * GROUP + 1, b]
+        for q in range(1, SIDE):
+            widest = jnp.maximum(widest, table_s[2 * GROUP, b + q])
+            largest = jnp.maximum(largest, table_s[2 * GROUP + 1, b + q])
+        plain = widest <= COPY
+
+        @pl.when(plain & (largest <= SMALL))
+        def _():
+            fast(b, SMALL)
+
+        @pl.when(plain & (largest > SMALL) & (largest <= LARGE))
+        def _():
+            fast(b, LARGE)
+
+        @pl.when(jnp.logical_not(plain) | (largest > LARGE))
+        def _():
+            lax.fori_loop(0, SIDE, lambda q, _: (slow(b + q), 0)[1], 0)
+
         return 0
 
-    lax.fori_loop(0, filled[2], long, 0)
+    lax.fori_loop(0, BLOCKS // SIDE, side, 0)
 
 
 def grid_kernel(
-    scale, row_block, lists_ref, out_ref, planes, flat, packed, keys, counts, turned, total,
-    counts_s, lists_s, sem, grid=None
+    scale, row_block, lists_ref, out_ref, planes, flat, packed, keys, table, turned, total, result,
+    table_s, sem, out_sems, *rest
 ):
     runs = lists_ref.shape[0]
     alone = runs == GROUP
+    buffers = rest[:SIDE]
+    grid = rest[SIDE] if not alone else None
 
     def finish(sums, inverse, rows):
         for c in range(CH):
@@ -227,10 +226,10 @@
                 grid[c, rows, :] += sums[c * BLOCK : (c + 1) * BLOCK]
 
     def group(g, _):
-        filled = merge_group(
-            g * GROUP, lists_ref, flat, packed, keys, counts, counts_s, lists_s, sem, alone
-        )
-        add_blocks(filled, packed, lists_s, total, emit)
+        copy = make_table(g * GROUP, lists_ref, keys, table, table_s, sem)
+        turn_runs(g * GROUP, lists_ref, flat)
+        copy.wait()
+        add_blocks(table_s, flat, buffers, packed, total, emit)
         return 0
 
     if alone:
@@ -255,6 +254,9 @@
         across = turned[slot, pl.ds(within, row_block), :]
         along = planes[p, pl.ds(first_row, row_block), :].astype(jnp.float32)
         return (0.5 * (along + across)).astype(jnp.bfloat16)
+
+    def sent(f):
+        return pltpu.make_async_copy(result.at[f], out_ref.at[f], out_sems.at[f])
 
     def frequency(f, slot):
         own = jnp.concatenate([own_rows(f, slot), own_rows(FB + f, slot + 1)], axis=0)
@@ -263,8 +265,9 @@
         by_real = jnp.dot(own, real, preferred_element_type=jnp.float32) + contract_last(own, real)
         by_imag = jnp.dot(own, imag, preferred_element_type=jnp.float32) + contract_last(own, imag)
         half = 0.5 * scale
-        out_ref[f, 0] = (by_real[:row_block] - by_imag[row_block:]) * half
-        out_ref[f, 1] = (by_imag[:row_block] + by_real[row_block:]) * half
+        result[f, 0] = (by_real[:row_block] - by_imag[row_block:]) * half
+        result[f, 1] = (by_imag[:row_block] + by_real[row_block:]) * half
+        sent(f).start()
 
     def pair(i, _):
         frequency(2 * i, 0)
@@ -272,6 +275,8 @@
         return 0
 
     lax.fori_loop(0, FB // 2, pair, 0)
+    for f in range(FB):
+        sent(f).wait()
 
 
 def whole(space=pltpu.VMEM):
@@ -306,26 +311,27 @@
     )
 
     traces = GROUP * count
-    slots = traces + BLOCKS * 8 + LARGE + COPY
     scratch = [
         pltpu.VMEM((CH, NG, NG), jnp.bfloat16),
         pltpu.VMEM((traces + COPY, 128), jnp.float32),
-        pltpu.VMEM((slots, 128), jnp.float32),
+        pltpu.VMEM((traces + LARGE, 128), jnp.float32),
         pltpu.VMEM((GROUP, count), jnp.float32),
-        pltpu.VMEM((GROUP + 8, 128), jnp.int32),
+        pltpu.VMEM((2 * GROUP + 8, 128), jnp.int32),
         pltpu.VMEM((4, 128, NG), jnp.float32),
         pltpu.VMEM(((CH + 1) * BLOCK, NG), jnp.float32),
-        pltpu.SMEM((GROUP + 8, 128), jnp.int32),
-        pltpu.SMEM((9, BLOCKS + UNROLL), jnp.int32),
+        pltpu.VMEM((FB, 2, row_block, NG), jnp.float32),
+        pltpu.SMEM((2 * GROUP + 8, 128), jnp.int32),
         pltpu.SemaphoreType.DMA,
+        pltpu.SemaphoreType.DMA((FB,)),
     ]
+    scratch += [pltpu.VMEM((LARGE + COPY, 128), jnp.float32)] * SIDE
     if runs != GROUP:
         scratch.append(pltpu.VMEM((CH + 1, NG, NG), jnp.float32))
     return pl.pallas_call(
         functools.partial(grid_kernel, 1.0 / math.sqrt(NG), row_block),
         out_shape=jax.ShapeDtypeStruct((FB, 2, row_block, NG), jnp.float32),
         in_specs=[whole()],
-        out_specs=whole(),
+        out_specs=whole(pl.ANY),
         scratch_shapes=scratch,
         compiler_params=params,
         name="grid",

time: 49 us -> 48.8 us (level); the launches traced: 48.7 us -> 47.9 us
  Pallas kernels: 27.8 us -> 26.9 us
    pallas_call x1, Pallas kernels: 25.1 us -> 24.2 us  [per_device(): pl.pallas_call(functools.partial(grid_kernel, 1.0 / math.sqrt(NG), row_bl...]
where the time goes in v4:
time: 48.8 us; the launch traced here: 47.9 us
  Pallas kernels  26.9 us (55%)
  blocking collectives  21 us (43%)
    pallas_call x1, Pallas kernels, per_device(): pl.pallas_call(functools.partial(grid_kernel, 1.0 / math.sqrt(NG), row_bl...  24.2 us
    all_to_all x1, blocking collectives, per_device(): lax.all_to_all(own.reshape(runs, ROWS, count), ('band', 'tile'), split_ax...  21 us
    pallas_call x1, Pallas kernels, per_device(): pl.pallas_call(functools.partial(run_kernel, cells_dev), out_shape=jax.Sh...  2.71 us

profile of v4, /device:TPU:0, one launch (start us, length us, event | category | flops | bytes accessed | tf_op | source)
XLA Modules:
  0.0 47.9 jit_solution(17610155390944373244)
XLA Ops:
  0.0 2.7 %own_run.1 = bf16[4,8,24,256]{3,2,1,0:T(8,128)(2,1)} custom-call(bf16[96,2048]{1,0:T(8,128)(2,1)} %constant.2.clone.twiddle_ref, bf16[1,256,2048]{2,1,0:T(8,128)(2,1)} %traces_ref.1, s32[1,1024]{1,0:T(1,128)} %bitcast.3, s32[1,1024]{1,0:T(1,128)} %offset_ref.1), custom_call_target="tpu_custom_call" | custom-call | tf_op jit(solution)/shard_map/own_run/pallas_call | solution.py:296
  2.7 21.0 %all_to_all.5.lists_ref = bf16[32,24,256]{2,1,0:T(8,128)(2,1)} all-to-all(bf16[32,24,256]{2,1,0:T(8,128)(2,1)} %bitcast.2), channel_id=1, replica_groups=mesh['band'=4,'tile'=8] {'band','tile'}, dimensions={0} | all-to-all | bytes 786432 | tf_op jit(solution)/shard_map/all_to_all | solution.py:309
  23.7 24.2 %grid.1 = f32[10,2,64,512]{3,2,1,0:T(8,128)} custom-call(bf16[32,24,256]{2,1,0:T(8,128)(2,1)} %all_to_all.5.lists_ref), custom_call_target="tpu_custom_call" | custom-call | tf_op jit(solution)/shard_map/grid/pallas_call | solution.py:330

commit v5 on v4

--- a/solution.py
+++ b/solution.py
@@ -19,8 +19,8 @@
 BLOCKS = NG // BLOCK
 GROUP = 32
 COPY = 32
-SMALL = 256
-LARGE = 512
+WIDTHS = (256, 512, 640)
+LARGE = WIDTHS[-1]
 SIDE = 4
 VMEM = 56 * 1024 * 1024
 
@@ -186,13 +186,14 @@
             largest = jnp.maximum(largest, table_s[2 * GROUP + 1, b + q])
         plain = widest <= COPY
 
-        @pl.when(plain & (largest <= SMALL))
-        def _():
-            fast(b, SMALL)
-
-        @pl.when(plain & (largest > SMALL) & (largest <= LARGE))
-        def _():
-            fast(b, LARGE)
+        least = -1
+        for width in WIDTHS:
+
+            @pl.when(plain & (largest > least) & (largest <= width))
+            def _(width=width):
+                fast(b, width)
+
+            least = width
 
         @pl.when(jnp.logical_not(plain) | (largest > LARGE))
         def _():

time: 48.8 us -> 42.5 us (0.87); the launches traced: 47.9 us -> 42.2 us
  Pallas kernels: 26.9 us -> 21.3 us
    pallas_call x1, Pallas kernels: 24.2 us -> 18.5 us  [per_device(): pl.pallas_call(functools.partial(grid_kernel, 1.0 / math.sqrt(NG), row_bl...]
where the time goes in v5:
time: 42.5 us; the launch traced here: 42.2 us
  Pallas kernels  21.3 us (50%)
  blocking collectives  21 us (49%)
    all_to_all x1, blocking collectives, per_device(): lax.all_to_all(own.reshape(runs, ROWS, count), ('band', 'tile'), split_ax...  21 us
    pallas_call x1, Pallas kernels, per_device(): pl.pallas_call(functools.partial(grid_kernel, 1.0 / math.sqrt(NG), row_bl...  18.5 us
    pallas_call x1, Pallas kernels, per_device(): pl.pallas_call(functools.partial(run_kernel, cells_dev), out_shape=jax.Sh...  2.71 us

profile of v5, /device:TPU:0, one launch (start us, length us, event | category | flops | bytes accessed | tf_op | source)
XLA Modules:
  0.0 42.2 jit_solution(6205926225997275816)
XLA Ops:
  0.0 2.7 %own_run.1 = bf16[4,8,24,256]{3,2,1,0:T(8,128)(2,1)} custom-call(bf16[96,2048]{1,0:T(8,128)(2,1)} %constant.2.clone.twiddle_ref, bf16[1,256,2048]{2,1,0:T(8,128)(2,1)} %traces_ref.1, s32[1,1024]{1,0:T(1,128)} %bitcast.3, s32[1,1024]{1,0:T(1,128)} %offset_ref.1), custom_call_target="tpu_custom_call" | custom-call | tf_op jit(solution)/shard_map/own_run/pallas_call | solution.py:297
  2.7 21.0 %all_to_all.5.lists_ref = bf16[32,24,256]{2,1,0:T(8,128)(2,1)} all-to-all(bf16[32,24,256]{2,1,0:T(8,128)(2,1)} %bitcast.2), channel_id=1, replica_groups=mesh['band'=4,'tile'=8] {'band','tile'}, dimensions={0} | all-to-all | bytes 786432 | tf_op jit(solution)/shard_map/all_to_all | solution.py:310
  23.7 18.5 %grid.1 = f32[10,2,64,512]{3,2,1,0:T(8,128)} custom-call(bf16[32,24,256]{2,1,0:T(8,128)(2,1)} %all_to_all.5.lists_ref), custom_call_target="tpu_custom_call" | custom-call | tf_op jit(solution)/shard_map/grid/pallas_call | solution.py:331

commit v6 on v5

--- a/solution.py
+++ b/solution.py
@@ -18,10 +18,10 @@
 BLOCK = 16
 BLOCKS = NG // BLOCK
 GROUP = 32
-COPY = 32
-WIDTHS = (256, 512, 640)
-LARGE = WIDTHS[-1]
+FORMS = ((16, 256), (32, 512), (32, 640))
+COPY, LARGE = FORMS[-1]
 SIDE = 4
+HALF = 256
 VMEM = 56 * 1024 * 1024
 
 
@@ -48,22 +48,25 @@
     cell = owner_ref[:, lanes] * cells_dev + offset_ref[:, lanes]
     order = cell * count + lax.broadcasted_iota(jnp.int32, (1, count), 1)
     rank = jnp.zeros((1, count), jnp.int32)
+    starts = jnp.zeros((1, count), jnp.int32)
+    limit = lax.broadcasted_iota(jnp.int32, (1, count), 1) * (BLOCK * NG * count)
+    limit = jnp.minimum(limit, NG * NG * count)
     for first in range(0, count, 128):
         column = jnp.transpose(jnp.broadcast_to(order[:, first : first + 128], (128, 128)))
         column = jnp.concatenate([column] * (count // 128), axis=1)
         rank += jnp.sum((column < order).astype(jnp.int32), axis=0, keepdims=True)
+        starts += jnp.sum((column < limit).astype(jnp.int32), axis=0, keepdims=True)
     target = lax.broadcasted_iota(jnp.int32, (count, count), 0)
     permute = (target == rank).astype(jnp.float32).astype(jnp.bfloat16)
     source = cell // NG
     receiver = cell % NG
     row = lax.broadcasted_iota(jnp.int32, (bands * ROWS, count), 0) % ROWS
-    digits = jnp.where(row == CH, source // BLOCK, 0)
-    digits = jnp.where(row == CH + 1, source % BLOCK, digits)
-    digits = jnp.where(row == CH + 2, receiver // 256, digits)
-    digits = jnp.where(row == CH + 3, receiver % 256, digits)
+    digits = jnp.where(row == CH + 1, source % BLOCK, 0)
+    digits = jnp.where(row == CH + 2, receiver // HALF, digits)
+    digits = jnp.where(row == CH + 3, receiver % HALF, digits)
     spectra = contract_last(twiddle_ref[...], traces_ref[0])
     packed = (spectra + digits.astype(jnp.float32)).astype(jnp.bfloat16)
-    ordered = contract_last(packed, permute)
+    ordered = contract_last(packed, permute) + jnp.where(row == CH, starts, 0).astype(jnp.float32)
     for band in range(bands):
         part = ordered[band * ROWS : (band + 1) * ROWS].astype(jnp.bfloat16)
         for tile in range(tiles):
@@ -73,13 +76,10 @@
 def make_table(first_run, lists_ref, keys, table, table_s, sem):
     length = lists_ref.shape[2]
     for r in range(GROUP):
-        keys[r : r + 1, :] = lists_ref[first_run + r].astype(jnp.float32)[CH : CH + 1]
-    block_of = keys[...]
+        part = lists_ref[first_run + r].astype(jnp.float32)
+        keys[r : r + 1, :] = part[CH : CH + 1, :128]
+    starts = keys[...]
     lane = lax.broadcasted_iota(jnp.int32, (GROUP, 128), 1)
-    starts = jnp.zeros((GROUP, 128), jnp.float32)
-    for b in range(1, BLOCKS + 1):
-        below = jnp.sum((block_of < float(b)).astype(jnp.float32), axis=1, keepdims=True)
-        starts = jnp.where(lane == b, below, starts)
     sizes = jnp.where(lane < BLOCKS, pltpu.roll(starts, 127, 1) - starts, 0.0)
     earlier = lax.broadcasted_iota(jnp.int32, (GROUP, GROUP), 0) > lax.broadcasted_iota(
         jnp.int32, (GROUP, GROUP), 1
@@ -110,7 +110,7 @@
             flat[at : at + 128, :ROWS] = jnp.transpose(part[:, first : first + 128])
 
 
-def product(first, size, width, packed):
+def products(first, size, width, packed):
     part = jnp.concatenate(
         [jnp.transpose(packed[pl.ds(first + k, 128), :])[:ROWS] for k in range(0, width, 128)],
         axis=1,
@@ -125,14 +125,15 @@
         return jnp.broadcast_to(row, (BLOCK, width)).astype(jnp.bfloat16)
 
     hit = spread(jnp.where(place < size, part[CH + 1 : CH + 2], -1.0)) == step
-    left = [jnp.where(hit, spread(part[c : c + 1]), none) for c in range(CH)]
-    left.append(jnp.where(hit, one, none))
-    right = []
-    for half in range(NG // 256):
+    left = [jnp.where(hit, one, none)]
+    left += [jnp.where(hit, spread(part[c : c + 1]), none) for c in range(CH)]
+    left = jnp.concatenate(left, axis=0)
+    for half in range(NG // HALF):
         low = spread(jnp.where(part[CH + 2 : CH + 3] == float(half), part[CH + 3 : CH + 4], -1.0))
-        for j in range(0, 256, BLOCK):
-            right.append(jnp.where(low == step + jnp.bfloat16(j), one, none))
-    return contract_last(jnp.concatenate(left, axis=0), jnp.concatenate(right, axis=0))
+        right = [
+            jnp.where(low == step + jnp.bfloat16(j), one, none) for j in range(0, HALF, BLOCK)
+        ]
+        yield pl.ds(half * HALF, HALF), contract_last(left, jnp.concatenate(right, axis=0))
 
 
 def block_rows(b):
@@ -140,17 +141,19 @@
 
 
 def add_blocks(table_s, flat, buffers, packed, total, emit):
-    def fast(b, width):
-        sums = []
+    def fast(b, rows, width):
+        def copies(q):
+            for r in range(GROUP):
+                buffers[q][pl.ds(table_s[GROUP + r, b + q], rows), :] = flat[
+                    pl.ds(table_s[r, b + q], rows), :
+                ]
+
+        copies(0)
         for q in range(SIDE):
-            buffer = buffers[q]
-            for r in range(GROUP):
-                buffer[pl.ds(table_s[GROUP + r, b + q], COPY), :] = flat[
-                    pl.ds(table_s[r, b + q], COPY), :
-                ]
-            sums.append(product(0, table_s[2 * GROUP + 1, b + q], width, buffer))
-        for q in range(SIDE):
-            emit(b + q, sums[q])
+            if q + 1 < SIDE:
+                copies(q + 1)
+            for lanes, sums in products(0, table_s[2 * GROUP + 1, b + q], width, buffers[q]):
+                emit(b + q, lanes, sums)
 
     def slow(b):
         def run(r, _):
@@ -171,11 +174,14 @@
 
         def piece(k, _):
             first = pl.multiple_of(k * LARGE, LARGE)
-            total[...] += product(first, size - first, LARGE, packed)
+            for lanes, sums in products(first, size - first, LARGE, packed):
+                total[:, lanes] += sums
             return 0
 
         lax.fori_loop(0, (size + LARGE - 1) // LARGE, piece, 0)
-        emit(b, total[...])
+        for half in range(NG // HALF):
+            lanes = pl.ds(half * HALF, HALF)
+            emit(b, lanes, total[:, lanes])
 
     def side(i, _):
         b = i * SIDE
@@ -184,18 +190,17 @@
         for q in range(1, SIDE):
             widest = jnp.maximum(widest, table_s[2 * GROUP, b + q])
             largest = jnp.maximum(largest, table_s[2 * GROUP + 1, b + q])
-        plain = widest <= COPY
-
-        least = -1
-        for width in WIDTHS:
-
-            @pl.when(plain & (largest > least) & (largest <= width))
-            def _(width=width):
-                fast(b, width)
-
-            least = width
-
-        @pl.when(jnp.logical_not(plain) | (largest > LARGE))
+        left_over = jnp.bool_(True)
+        for rows, width in FORMS:
+            fits = (widest <= rows) & (largest <= width)
+
+            @pl.when(left_over & fits)
+            def _(rows=rows, width=width):
+                fast(b, rows, width)
+
+            left_over = left_over & jnp.logical_not(fits)
+
+        @pl.when(left_over)
         def _():
             lax.fori_loop(0, SIDE, lambda q, _: (slow(b + q), 0)[1], 0)
 
@@ -213,18 +218,18 @@
     buffers = rest[:SIDE]
     grid = rest[SIDE] if not alone else None
 
-    def finish(sums, inverse, rows):
+    def finish(sums, rows, lanes):
+        inverse = 1.0 / jnp.maximum(sums(0), 1.0)
         for c in range(CH):
-            planes[c, rows, :] = (sums(c) * inverse).astype(jnp.bfloat16)
-
-    def emit(b, sums):
+            planes[c, rows, lanes] = (sums(c + 1) * inverse).astype(jnp.bfloat16)
+
+    def emit(b, lanes, sums):
         rows = block_rows(b)
         if alone:
-            inverse = 1.0 / jnp.maximum(sums[CH * BLOCK :], 1.0)
-            finish(lambda c: sums[c * BLOCK : (c + 1) * BLOCK], inverse, rows)
+            finish(lambda c: sums[c * BLOCK : (c + 1) * BLOCK], rows, lanes)
         else:
             for c in range(CH + 1):
-                grid[c, rows, :] += sums[c * BLOCK : (c + 1) * BLOCK]
+                grid[c, rows, lanes] += sums[c * BLOCK : (c + 1) * BLOCK]
 
     def group(g, _):
         copy = make_table(g * GROUP, lists_ref, keys, table, table_s, sem)
@@ -241,7 +246,7 @@
 
         def divide(b, _):
             rows = block_rows(b)
-            finish(lambda c: grid[c, rows, :], 1.0 / jnp.maximum(grid[CH, rows, :], 1.0), rows)
+            finish(lambda c: grid[c, rows, :], rows, pl.ds(0, NG))
             return 0
 
         lax.fori_loop(0, BLOCKS, divide, 0)
@@ -316,7 +321,7 @@
         pltpu.VMEM((CH, NG, NG), jnp.bfloat16),
         pltpu.VMEM((traces + COPY, 128), jnp.float32),
         pltpu.VMEM((traces + LARGE, 128), jnp.float32),
-        pltpu.VMEM((GROUP, count), jnp.float32),
+        pltpu.VMEM((GROUP, 128), jnp.float32),
         pltpu.VMEM((2 * GROUP + 8, 128), jnp.int32),
         pltpu.VMEM((4, 128, NG), jnp.float32),
         pltpu.VMEM(((CH + 1) * BLOCK, NG), jnp.float32),

time: 42.5 us -> 41.5 us (0.976)
  Pallas kernels: 21.3 us -> 20.3 us
    pallas_call x1, Pallas kernels: 18.5 us -> 17.6 us  [per_device(): pl.pallas_call(functools.partial(grid_kernel, 1.0 / math.sqrt(NG), row_bl...]
where the time goes in v6:
time: 41.5 us; the launch traced here: 41.3 us
  blocking collectives  21 us (51%)
  Pallas kernels  20.3 us (49%)
    all_to_all x1, blocking collectives, per_device(): lax.all_to_all(own.reshape(runs, ROWS, count), ('band', 'tile'), split_ax...  21 us
    pallas_call x1, Pallas kernels, per_device(): pl.pallas_call(functools.partial(grid_kernel, 1.0 / math.sqrt(NG), row_bl...  17.6 us
    pallas_call x1, Pallas kernels, per_device(): pl.pallas_call(functools.partial(run_kernel, cells_dev), out_shape=jax.Sh...  2.71 us

profile of v6, /device:TPU:0, one launch (start us, length us, event | category | flops | bytes accessed | tf_op | source)
XLA Modules:
  0.0 41.3 jit_solution(9334099071077701509)
XLA Ops:
  0.0 2.7 %own_run.1 = bf16[4,8,24,256]{3,2,1,0:T(8,128)(2,1)} custom-call(bf16[96,2048]{1,0:T(8,128)(2,1)} %constant.2.clone.twiddle_ref, bf16[1,256,2048]{2,1,0:T(8,128)(2,1)} %traces_ref.1, s32[1,1024]{1,0:T(1,128)} %bitcast.3, s32[1,1024]{1,0:T(1,128)} %offset_ref.1), custom_call_target="tpu_custom_call" | custom-call | tf_op jit(solution)/shard_map/own_run/pallas_call | solution.py:302
  2.7 21.0 %all_to_all.5.lists_ref = bf16[32,24,256]{2,1,0:T(8,128)(2,1)} all-to-all(bf16[32,24,256]{2,1,0:T(8,128)(2,1)} %bitcast.2), channel_id=1, replica_groups=mesh['band'=4,'tile'=8] {'band','tile'}, dimensions={0} | all-to-all | bytes 786432 | tf_op jit(solution)/shard_map/all_to_all | solution.py:315
  23.7 17.6 %grid.1 = f32[10,2,64,512]{3,2,1,0:T(8,128)} custom-call(bf16[32,24,256]{2,1,0:T(8,128)(2,1)} %all_to_all.5.lists_ref), custom_call_target="tpu_custom_call" | custom-call | tf_op jit(solution)/shard_map/grid/pallas_call | solution.py:336

commit v7 on v6

--- a/solution.py
+++ b/solution.py
@@ -20,7 +20,7 @@
 GROUP = 32
 FORMS = ((16, 256), (32, 512), (32, 640))
 COPY, LARGE = FORMS[-1]
-SIDE = 4
+SIDE = 2
 HALF = 256
 VMEM = 56 * 1024 * 1024
 

time: 41.5 us -> 43.9 us (1.058)
  Pallas kernels: 20.3 us -> 22.6 us
    pallas_call x1, Pallas kernels: 17.6 us -> 19.9 us  [per_device(): pl.pallas_call(functools.partial(grid_kernel, 1.0 / math.sqrt(NG), row_bl...]
where the time goes in v7:
time: 43.9 us; the launch traced here: 43.6 us
  Pallas kernels  22.6 us (51%)
  blocking collectives  21 us (48%)
    all_to_all x1, blocking collectives, per_device(): lax.all_to_all(own.reshape(runs, ROWS, count), ('band', 'tile'), split_ax...  21 us
    pallas_call x1, Pallas kernels, per_device(): pl.pallas_call(functools.partial(grid_kernel, 1.0 / math.sqrt(NG), row_bl...  19.9 us
    pallas_call x1, Pallas kernels, per_device(): pl.pallas_call(functools.partial(run_kernel, cells_dev), out_shape=jax.Sh...  2.71 us

profile of v7, /device:TPU:0, one launch (start us, length us, event | category | flops | bytes accessed | tf_op | source)
XLA Modules:
  0.0 43.6 jit_solution(2094330462042439610)
XLA Ops:
  0.0 2.7 %own_run.1 = bf16[4,8,24,256]{3,2,1,0:T(8,128)(2,1)} custom-call(bf16[96,2048]{1,0:T(8,128)(2,1)} %constant.2.clone.twiddle_ref, bf16[1,256,2048]{2,1,0:T(8,128)(2,1)} %traces_ref.1, s32[1,1024]{1,0:T(1,128)} %bitcast.3, s32[1,1024]{1,0:T(1,128)} %offset_ref.1), custom_call_target="tpu_custom_call" | custom-call | tf_op jit(solution)/shard_map/own_run/pallas_call | solution.py:302
  2.7 21.0 %all_to_all.5.lists_ref = bf16[32,24,256]{2,1,0:T(8,128)(2,1)} all-to-all(bf16[32,24,256]{2,1,0:T(8,128)(2,1)} %bitcast.2), channel_id=1, replica_groups=mesh['band'=4,'tile'=8] {'band','tile'}, dimensions={0} | all-to-all | bytes 786432 | tf_op jit(solution)/shard_map/all_to_all | solution.py:315
  23.7 19.9 %grid.1 = f32[10,2,64,512]{3,2,1,0:T(8,128)} custom-call(bf16[32,24,256]{2,1,0:T(8,128)(2,1)} %all_to_all.5.lists_ref), custom_call_target="tpu_custom_call" | custom-call | tf_op jit(solution)/shard_map/grid/pallas_call | solution.py:336

commit v8 on v6

--- a/solution.py
+++ b/solution.py
@@ -20,6 +20,7 @@
 GROUP = 32
 FORMS = ((16, 256), (32, 512), (32, 640))
 COPY, LARGE = FORMS[-1]
+BESIDE = 5
 SIDE = 4
 HALF = 256
 VMEM = 56 * 1024 * 1024
@@ -275,12 +276,12 @@
         result[f, 1] = (by_imag[:row_block] + by_real[row_block:]) * half
         sent(f).start()
 
-    def pair(i, _):
-        frequency(2 * i, 0)
-        frequency(2 * i + 1, 2)
+    def some(i, _):
+        for q in range(BESIDE):
+            frequency(i * BESIDE + q, 2 * q)
         return 0
 
-    lax.fori_loop(0, FB // 2, pair, 0)
+    lax.fori_loop(0, FB // BESIDE, some, 0)
     for f in range(FB):
         sent(f).wait()
 
@@ -323,7 +324,7 @@
         pltpu.VMEM((traces + LARGE, 128), jnp.float32),
         pltpu.VMEM((GROUP, 128), jnp.float32),
         pltpu.VMEM((2 * GROUP + 8, 128), jnp.int32),
-        pltpu.VMEM((4, 128, NG), jnp.float32),
+        pltpu.VMEM((2 * BESIDE, 128, NG), jnp.float32),
         pltpu.VMEM(((CH + 1) * BLOCK, NG), jnp.float32),
         pltpu.VMEM((FB, 2, row_block, NG), jnp.float32),
         pltpu.SMEM((2 * GROUP + 8, 128), jnp.int32),

time: 41.5 us -> 40.8 us (0.983)
  Pallas kernels: 20.3 us -> 19.5 us
    pallas_call x1, Pallas kernels: 17.6 us -> 16.8 us  [per_device(): pl.pallas_call(functools.partial(grid_kernel, 1.0 / math.sqrt(NG), row_bl...]
where the time goes in v8:
time: 40.8 us; the launch traced here: 40.5 us
  blocking collectives  21 us (51%)
  Pallas kernels  19.5 us (48%)
    all_to_all x1, blocking collectives, per_device(): lax.all_to_all(own.reshape(runs, ROWS, count), ('band', 'tile'), split_ax...  21 us
    pallas_call x1, Pallas kernels, per_device(): pl.pallas_call(functools.partial(grid_kernel, 1.0 / math.sqrt(NG), row_bl...  16.8 us
    pallas_call x1, Pallas kernels, per_device(): pl.pallas_call(functools.partial(run_kernel, cells_dev), out_shape=jax.Sh...  2.71 us

profile of v8, /device:TPU:0, one launch (start us, length us, event | category | flops | bytes accessed | tf_op | source)
XLA Modules:
  0.0 40.5 jit_solution(10204260756492943309)
XLA Ops:
  0.0 2.7 %own_run.1 = bf16[4,8,24,256]{3,2,1,0:T(8,128)(2,1)} custom-call(bf16[96,2048]{1,0:T(8,128)(2,1)} %constant.2.clone.twiddle_ref, bf16[1,256,2048]{2,1,0:T(8,128)(2,1)} %traces_ref.1, s32[1,1024]{1,0:T(1,128)} %bitcast.3, s32[1,1024]{1,0:T(1,128)} %offset_ref.1), custom_call_target="tpu_custom_call" | custom-call | tf_op jit(solution)/shard_map/own_run/pallas_call | solution.py:303
  2.7 21.0 %all_to_all.5.lists_ref = bf16[32,24,256]{2,1,0:T(8,128)(2,1)} all-to-all(bf16[32,24,256]{2,1,0:T(8,128)(2,1)} %bitcast.2), channel_id=1, replica_groups=mesh['band'=4,'tile'=8] {'band','tile'}, dimensions={0} | all-to-all | bytes 786432 | tf_op jit(solution)/shard_map/all_to_all | solution.py:316
  23.7 16.8 %grid.1 = f32[10,2,64,512]{3,2,1,0:T(8,128)} custom-call(bf16[32,24,256]{2,1,0:T(8,128)(2,1)} %all_to_all.5.lists_ref), custom_call_target="tpu_custom_call" | custom-call | tf_op jit(solution)/shard_map/grid/pallas_call | solution.py:337

commit v9 on v8

--- a/solution.py
+++ b/solution.py
@@ -20,7 +20,7 @@
 GROUP = 32
 FORMS = ((16, 256), (32, 512), (32, 640))
 COPY, LARGE = FORMS[-1]
-BESIDE = 5
+BESIDE = 2
 SIDE = 4
 HALF = 256
 VMEM = 56 * 1024 * 1024
@@ -211,7 +211,7 @@
 
 
 def grid_kernel(
-    scale, row_block, lists_ref, out_ref, planes, flat, packed, keys, table, turned, total, result,
+    scale, row_block, lists_ref, out_ref, planes, flat, packed, keys, table, twice, total, result,
     table_s, sem, out_sems, *rest
 ):
     runs = lists_ref.shape[0]
@@ -252,28 +252,21 @@
 
         lax.fori_loop(0, BLOCKS, divide, 0)
 
-    first_row = pl.multiple_of(lax.axis_index("tile") * row_block, row_block)
-    first_col = pl.multiple_of(first_row // 128 * 128, 128)
-    within = pl.multiple_of(first_row % 128, row_block)
-
-    def own_rows(p, slot):
-        turned[slot] = jnp.transpose(planes[p, :, pl.ds(first_col, 128)].astype(jnp.float32))
-        across = turned[slot, pl.ds(within, row_block), :]
-        along = planes[p, pl.ds(first_row, row_block), :].astype(jnp.float32)
-        return (0.5 * (along + across)).astype(jnp.bfloat16)
+    own_rows = pl.ds(pl.multiple_of(lax.axis_index("tile") * row_block, row_block), row_block)
 
     def sent(f):
         return pltpu.make_async_copy(result.at[f], out_ref.at[f], out_sems.at[f])
 
     def frequency(f, slot):
-        own = jnp.concatenate([own_rows(f, slot), own_rows(FB + f, slot + 1)], axis=0)
-        real = planes[f]
-        imag = planes[FB + f]
-        by_real = jnp.dot(own, real, preferred_element_type=jnp.float32) + contract_last(own, real)
-        by_imag = jnp.dot(own, imag, preferred_element_type=jnp.float32) + contract_last(own, imag)
-        half = 0.5 * scale
-        result[f, 0] = (by_real[:row_block] - by_imag[row_block:]) * half
-        result[f, 1] = (by_imag[:row_block] + by_real[row_block:]) * half
+        for part, p in enumerate((f, FB + f)):
+            plane = planes[p]
+            twice[slot + part] = plane + jnp.transpose(plane)
+        own = jnp.concatenate([twice[slot, own_rows, :], twice[slot + 1, own_rows, :]], axis=0)
+        by_real = jnp.dot(own, twice[slot], preferred_element_type=jnp.float32)
+        by_imag = jnp.dot(own, twice[slot + 1], preferred_element_type=jnp.float32)
+        quarter = 0.25 * scale
+        result[f, 0] = (by_real[:row_block] - by_imag[row_block:]) * quarter
+        result[f, 1] = (by_imag[:row_block] + by_real[row_block:]) * quarter
         sent(f).start()
 
     def some(i, _):
@@ -324,7 +317,7 @@
         pltpu.VMEM((traces + LARGE, 128), jnp.float32),
         pltpu.VMEM((GROUP, 128), jnp.float32),
         pltpu.VMEM((2 * GROUP + 8, 128), jnp.int32),
-        pltpu.VMEM((2 * BESIDE, 128, NG), jnp.float32),
+        pltpu.VMEM((2 * BESIDE, NG, NG), jnp.bfloat16),
         pltpu.VMEM(((CH + 1) * BLOCK, NG), jnp.float32),
         pltpu.VMEM((FB, 2, row_block, NG), jnp.float32),
         pltpu.SMEM((2 * GROUP + 8, 128), jnp.int32),

time: 40.8 us -> 39.8 us (0.975)
  Pallas kernels: 19.5 us -> 18.4 us
    pallas_call x1, Pallas kernels: 16.8 us -> 15.7 us  [per_device(): pl.pallas_call(functools.partial(grid_kernel, 1.0 / math.sqrt(NG), row_bl...]
where the time goes in v9:
time: 39.8 us; the launch traced here: 39.4 us
  blocking collectives  21 us (53%)
  Pallas kernels  18.4 us (46%)
    all_to_all x1, blocking collectives, per_device(): lax.all_to_all(own.reshape(runs, ROWS, count), ('band', 'tile'), split_ax...  21 us
    pallas_call x1, Pallas kernels, per_device(): pl.pallas_call(functools.partial(grid_kernel, 1.0 / math.sqrt(NG), row_bl...  15.7 us
    pallas_call x1, Pallas kernels, per_device(): pl.pallas_call(functools.partial(run_kernel, cells_dev), out_shape=jax.Sh...  2.71 us

profile of v9, /device:TPU:0, one launch (start us, length us, event | category | flops | bytes accessed | tf_op | source)
XLA Modules:
  0.0 39.4 jit_solution(15148254351717431072)
XLA Ops:
  0.0 2.7 %own_run.1 = bf16[4,8,24,256]{3,2,1,0:T(8,128)(2,1)} custom-call(bf16[96,2048]{1,0:T(8,128)(2,1)} %constant.2.clone.twiddle_ref, bf16[1,256,2048]{2,1,0:T(8,128)(2,1)} %traces_ref.1, s32[1,1024]{1,0:T(1,128)} %bitcast.3, s32[1,1024]{1,0:T(1,128)} %offset_ref.1), custom_call_target="tpu_custom_call" | custom-call | tf_op jit(solution)/shard_map/own_run/pallas_call | solution.py:296
  2.7 21.0 %all_to_all.5.lists_ref = bf16[32,24,256]{2,1,0:T(8,128)(2,1)} all-to-all(bf16[32,24,256]{2,1,0:T(8,128)(2,1)} %bitcast.2), channel_id=1, replica_groups=mesh['band'=4,'tile'=8] {'band','tile'}, dimensions={0} | all-to-all | bytes 786432 | tf_op jit(solution)/shard_map/all_to_all | solution.py:309
  23.7 15.7 %grid.1 = f32[10,2,64,512]{3,2,1,0:T(8,128)} custom-call(bf16[32,24,256]{2,1,0:T(8,128)(2,1)} %all_to_all.5.lists_ref), custom_call_target="tpu_custom_call" | custom-call | tf_op jit(solution)/shard_map/grid/pallas_call | solution.py:330

commit v10 on v9

--- a/solution.py
+++ b/solution.py
@@ -18,8 +18,9 @@
 BLOCK = 16
 BLOCKS = NG // BLOCK
 GROUP = 32
-FORMS = ((16, 256), (32, 512), (32, 640))
-COPY, LARGE = FORMS[-1]
+COPY = 32
+WIDTHS = (256, 512, 640)
+LARGE = WIDTHS[-1]
 BESIDE = 2
 SIDE = 4
 HALF = 256
@@ -92,7 +93,7 @@
     )
     run = lax.broadcasted_iota(jnp.int32, (GROUP, 128), 0)
     table[:GROUP, :] = starts.astype(jnp.int32) + run * length
-    table[GROUP : 2 * GROUP, :] = targets.astype(jnp.int32)
+    table[GROUP : 2 * GROUP, :] = jnp.minimum(targets, float(LARGE)).astype(jnp.int32)
     widest = jnp.max(sizes, axis=0, keepdims=True)
     total = jnp.sum(sizes, axis=0, keepdims=True)
     last = lax.broadcasted_iota(jnp.int32, (8, 128), 0)
@@ -111,11 +112,15 @@
             flat[at : at + 128, :ROWS] = jnp.transpose(part[:, first : first + 128])
 
 
-def products(first, size, width, packed):
-    part = jnp.concatenate(
+def turned(first, width, packed):
+    return jnp.concatenate(
         [jnp.transpose(packed[pl.ds(first + k, 128), :])[:ROWS] for k in range(0, width, 128)],
         axis=1,
     )
+
+
+def products(part, size):
+    width = part.shape[1]
     step = lax.broadcasted_iota(jnp.int32, (BLOCK, width), 0).astype(jnp.float32)
     step = step.astype(jnp.bfloat16)
     place = lax.broadcasted_iota(jnp.int32, (1, width), 1)
@@ -141,33 +146,33 @@
     return pl.ds(pl.multiple_of(b * BLOCK, BLOCK), BLOCK)
 
 
-def add_blocks(table_s, flat, buffers, packed, total, emit):
-    def fast(b, rows, width):
-        def copies(q):
-            for r in range(GROUP):
-                buffers[q][pl.ds(table_s[GROUP + r, b + q], rows), :] = flat[
-                    pl.ds(table_s[r, b + q], rows), :
-                ]
-
-        copies(0)
+def add_blocks(table_s, flat, buffers, now, later, packed, total, emit):
+    sides = BLOCKS // SIDE
+
+    def merge(i, q):
+        b = jnp.minimum(i, sides - 1) * SIDE + q
+        for r in range(GROUP):
+            buffers[q][pl.ds(table_s[GROUP + r, b], COPY), :] = flat[pl.ds(table_s[r, b], COPY), :]
+        later[q] = turned(0, LARGE, buffers[q])
+
+    def fast(i, width):
         for q in range(SIDE):
-            if q + 1 < SIDE:
-                copies(q + 1)
-            for lanes, sums in products(0, table_s[2 * GROUP + 1, b + q], width, buffers[q]):
-                emit(b + q, lanes, sums)
+            merge(i + 1, q)
+            b = i * SIDE + q
+            for lanes, sums in products(now[q, :, :width], table_s[2 * GROUP + 1, b]):
+                emit(b, lanes, sums)
 
     def slow(b):
-        def run(r, _):
+        def run(r, target):
             source = table_s[r, b]
-            target = table_s[GROUP + r, b]
-            after = table_s[2 * GROUP + 1, b]
-            after = jnp.where(r + 1 < GROUP, table_s[jnp.minimum(GROUP + r + 1, 2 * GROUP - 1), b], after)
+            count = table_s[r, b + 1] - source
 
             def piece(k, _):
                 packed[pl.ds(target + 8 * k, 8), :] = flat[pl.ds(source + 8 * k, 8), :]
                 return 0
 
-            return lax.fori_loop(0, (after - target + 7) // 8, piece, 0)
+            lax.fori_loop(0, (count + 7) // 8, piece, 0)
+            return target + count
 
         lax.fori_loop(0, GROUP, run, 0)
         total[...] = jnp.zeros_like(total)
@@ -175,7 +180,7 @@
 
         def piece(k, _):
             first = pl.multiple_of(k * LARGE, LARGE)
-            for lanes, sums in products(first, size - first, LARGE, packed):
+            for lanes, sums in products(turned(first, LARGE, packed), size - first):
                 total[:, lanes] += sums
             return 0
 
@@ -191,23 +196,28 @@
         for q in range(1, SIDE):
             widest = jnp.maximum(widest, table_s[2 * GROUP, b + q])
             largest = jnp.maximum(largest, table_s[2 * GROUP + 1, b + q])
-        left_over = jnp.bool_(True)
-        for rows, width in FORMS:
-            fits = (widest <= rows) & (largest <= width)
-
-            @pl.when(left_over & fits)
-            def _(rows=rows, width=width):
-                fast(b, rows, width)
-
-            left_over = left_over & jnp.logical_not(fits)
-
-        @pl.when(left_over)
+        now[...] = later[...]
+        plain = widest <= COPY
+        least = -1
+        for width in WIDTHS:
+
+            @pl.when(plain & (largest > least) & (largest <= width))
+            def _(width=width):
+                fast(i, width)
+
+            least = width
+
+        @pl.when(jnp.logical_not(plain) | (largest > LARGE))
         def _():
+            for q in range(SIDE):
+                merge(i + 1, q)
             lax.fori_loop(0, SIDE, lambda q, _: (slow(b + q), 0)[1], 0)
 
         return 0
 
-    lax.fori_loop(0, BLOCKS // SIDE, side, 0)
+    for q in range(SIDE):
+        merge(jnp.int32(0), q)
+    lax.fori_loop(0, sides, side, 0)
 
 
 def grid_kernel(
@@ -216,8 +226,8 @@
 ):
     runs = lists_ref.shape[0]
     alone = runs == GROUP
-    buffers = rest[:SIDE]
-    grid = rest[SIDE] if not alone else None
+    now, later, *buffers = rest[: SIDE + 2]
+    grid = rest[SIDE + 2] if not alone else None
 
     def finish(sums, rows, lanes):
         inverse = 1.0 / jnp.maximum(sums(0), 1.0)
@@ -236,7 +246,7 @@
         copy = make_table(g * GROUP, lists_ref, keys, table, table_s, sem)
         turn_runs(g * GROUP, lists_ref, flat)
         copy.wait()
-        add_blocks(table_s, flat, buffers, packed, total, emit)
+        add_blocks(table_s, flat, buffers, now, later, packed, total, emit)
         return 0
 
     if alone:
@@ -324,6 +334,7 @@
         pltpu.SemaphoreType.DMA,
         pltpu.SemaphoreType.DMA((FB,)),
     ]
+    scratch += [pltpu.VMEM((SIDE, ROWS, LARGE), jnp.float32)] * 2
     scratch += [pltpu.VMEM((LARGE + COPY, 128), jnp.float32)] * SIDE
     if runs != GROUP:
         scratch.append(pltpu.VMEM((CH + 1, NG, NG), jnp.float32))

time: 39.8 us -> 39.2 us (0.985)
  no operation moved by 1% of the time
where the time goes in v10:
time: 39.2 us; the launch traced here: 39.1 us
  blocking collectives  21 us (54%)
  Pallas kernels  18.2 us (46%)
    all_to_all x1, blocking collectives, per_device(): lax.all_to_all(own.reshape(runs, ROWS, count), ('band', 'tile'), split_ax...  21 us
    pallas_call x1, Pallas kernels, per_device(): pl.pallas_call(functools.partial(grid_kernel, 1.0 / math.sqrt(NG), row_bl...  15.4 us
    pallas_call x1, Pallas kernels, per_device(): pl.pallas_call(functools.partial(run_kernel, cells_dev), out_shape=jax.Sh...  2.71 us

profile of v10, /device:TPU:0, one launch (start us, length us, event | category | flops | bytes accessed | tf_op | source)
XLA Modules:
  0.0 39.1 jit_solution(17594084722842272122)
XLA Ops:
  0.0 2.7 %own_run.1 = bf16[4,8,24,256]{3,2,1,0:T(8,128)(2,1)} custom-call(bf16[96,2048]{1,0:T(8,128)(2,1)} %constant.2.clone.twiddle_ref, bf16[1,256,2048]{2,1,0:T(8,128)(2,1)} %traces_ref.1, s32[1,1024]{1,0:T(1,128)} %bitcast.3, s32[1,1024]{1,0:T(1,128)} %offset_ref.1), custom_call_target="tpu_custom_call" | custom-call | tf_op jit(solution)/shard_map/own_run/pallas_call | solution.py:306
  2.7 21.0 %all_to_all.5.lists_ref = bf16[32,24,256]{2,1,0:T(8,128)(2,1)} all-to-all(bf16[32,24,256]{2,1,0:T(8,128)(2,1)} %bitcast.2), channel_id=1, replica_groups=mesh['band'=4,'tile'=8] {'band','tile'}, dimensions={0} | all-to-all | bytes 786432 | tf_op jit(solution)/shard_map/all_to_all | solution.py:319
  23.7 15.4 %grid.1 = f32[10,2,64,512]{3,2,1,0:T(8,128)} custom-call(bf16[32,24,256]{2,1,0:T(8,128)(2,1)} %all_to_all.5.lists_ref), custom_call_target="tpu_custom_call" | custom-call | tf_op jit(solution)/shard_map/grid/pallas_call | solution.py:341

commit v11 on v10

--- a/solution.py
+++ b/solution.py
@@ -21,8 +21,9 @@
 COPY = 32
 WIDTHS = (256, 512, 640)
 LARGE = WIDTHS[-1]
-BESIDE = 2
+BESIDE = 5
 SIDE = 4
+PIECES = 4
 HALF = 256
 VMEM = 56 * 1024 * 1024
 
@@ -44,7 +45,24 @@
     )
 
 
-def run_kernel(cells_dev, twiddle_ref, traces_ref, owner_ref, offset_ref, out_ref):
+def run_kernel(
+    cells_dev, twiddle_ref, traces_ref, owner_ref, offset_ref, out_ref, twiddle, traces, sems
+):
+    width = traces.shape[1] // PIECES
+    pieces = []
+    for k in range(PIECES):
+        columns = pl.ds(k * width, width)
+        pair = (
+            pltpu.make_async_copy(
+                twiddle_ref.at[:, columns], twiddle.at[:, columns], sems.at[0, k]
+            ),
+            pltpu.make_async_copy(
+                traces_ref.at[0, :, columns], traces.at[:, columns], sems.at[1, k]
+            ),
+        )
+        for copy in pair:
+            copy.start()
+        pieces.append(pair)
     bands, tiles, _, count = out_ref.shape
     lanes = pl.ds(pl.multiple_of(lax.axis_index("band") * count, count), count)
     cell = owner_ref[:, lanes] * cells_dev + offset_ref[:, lanes]
@@ -66,7 +84,12 @@
     digits = jnp.where(row == CH + 1, source % BLOCK, 0)
     digits = jnp.where(row == CH + 2, receiver // HALF, digits)
     digits = jnp.where(row == CH + 3, receiver % HALF, digits)
-    spectra = contract_last(twiddle_ref[...], traces_ref[0])
+    spectra = jnp.zeros((bands * ROWS, count), jnp.float32)
+    for k in range(PIECES):
+        for copy in pieces[k]:
+            copy.wait()
+        columns = pl.ds(k * width, width)
+        spectra += contract_last(twiddle[:, columns], traces[:, columns])
     packed = (spectra + digits.astype(jnp.float32)).astype(jnp.bfloat16)
     ordered = contract_last(packed, permute) + jnp.where(row == CH, starts, 0).astype(jnp.float32)
     for band in range(bands):
@@ -146,7 +169,7 @@
     return pl.ds(pl.multiple_of(b * BLOCK, BLOCK), BLOCK)
 
 
-def add_blocks(table_s, flat, buffers, now, later, packed, total, emit):
+def add_blocks(table_s, flat, buffers, later, packed, total, emit):
     sides = BLOCKS // SIDE
 
     def merge(i, q):
@@ -156,10 +179,11 @@
         later[q] = turned(0, LARGE, buffers[q])
 
     def fast(i, width):
+        parts = [later[q, :, :width] for q in range(SIDE)]
         for q in range(SIDE):
             merge(i + 1, q)
             b = i * SIDE + q
-            for lanes, sums in products(now[q, :, :width], table_s[2 * GROUP + 1, b]):
+            for lanes, sums in products(parts[q], table_s[2 * GROUP + 1, b]):
                 emit(b, lanes, sums)
 
     def slow(b):
@@ -196,7 +220,6 @@
         for q in range(1, SIDE):
             widest = jnp.maximum(widest, table_s[2 * GROUP, b + q])
             largest = jnp.maximum(largest, table_s[2 * GROUP + 1, b + q])
-        now[...] = later[...]
         plain = widest <= COPY
         least = -1
         for width in WIDTHS:
@@ -226,8 +249,8 @@
 ):
     runs = lists_ref.shape[0]
     alone = runs == GROUP
-    now, later, *buffers = rest[: SIDE + 2]
-    grid = rest[SIDE + 2] if not alone else None
+    later, *buffers = rest[: SIDE + 1]
+    grid = rest[SIDE + 1] if not alone else None
 
     def finish(sums, rows, lanes):
         inverse = 1.0 / jnp.maximum(sums(0), 1.0)
@@ -246,7 +269,7 @@
         copy = make_table(g * GROUP, lists_ref, keys, table, table_s, sem)
         turn_runs(g * GROUP, lists_ref, flat)
         copy.wait()
-        add_blocks(table_s, flat, buffers, now, later, packed, total, emit)
+        add_blocks(table_s, flat, buffers, later, packed, total, emit)
         return 0
 
     if alone:
@@ -306,8 +329,13 @@
     own = pl.pallas_call(
         functools.partial(run_kernel, cells_dev),
         out_shape=jax.ShapeDtypeStruct((band_count, tile_count, ROWS, count), jnp.bfloat16),
-        in_specs=[whole()] * 4,
+        in_specs=[whole(pl.ANY)] * 2 + [whole()] * 2,
         out_specs=whole(),
+        scratch_shapes=[
+            pltpu.VMEM((runs * ROWS // tile_count, NT), jnp.bfloat16),
+            pltpu.VMEM((count, NT), jnp.bfloat16),
+            pltpu.SemaphoreType.DMA((2, PIECES)),
+        ],
         compiler_params=params,
         name="own_run",
     )(
@@ -334,7 +362,7 @@
         pltpu.SemaphoreType.DMA,
         pltpu.SemaphoreType.DMA((FB,)),
     ]
-    scratch += [pltpu.VMEM((SIDE, ROWS, LARGE), jnp.float32)] * 2
+    scratch.append(pltpu.VMEM((SIDE, ROWS, LARGE), jnp.float32))
     scratch += [pltpu.VMEM((LARGE + COPY, 128), jnp.float32)] * SIDE
     if runs != GROUP:
         scratch.append(pltpu.VMEM((CH + 1, NG, NG), jnp.float32))

time: 39.2 us -> 39.2 us (level)
    pallas_call x1, Pallas kernels: 15.4 us -> 14.3 us  [per_device(): pl.pallas_call(functools.partial(grid_kernel, 1.0 / math.sqrt(NG), row_bl...]
    pallas_call x1, Pallas kernels: 2.71 us -> 3.59 us  [per_device(): pl.pallas_call(functools.partial(run_kernel, cells_dev), out_shape=jax.Sh...]
where the time goes in v11:
time: 39.2 us; the launch traced here: 38.9 us
  blocking collectives  21 us (54%)
  Pallas kernels  17.9 us (46%)
    all_to_all x1, blocking collectives, per_device(): lax.all_to_all(own.reshape(runs, ROWS, count), ('band', 'tile'), split_ax...  21 us
    pallas_call x1, Pallas kernels, per_device(): pl.pallas_call(functools.partial(grid_kernel, 1.0 / math.sqrt(NG), row_bl...  14.3 us
    pallas_call x1, Pallas kernels, per_device(): pl.pallas_call(functools.partial(run_kernel, cells_dev), out_shape=jax.Sh...  3.59 us

profile of v11, /device:TPU:0, one launch (start us, length us, event | category | flops | bytes accessed | tf_op | source)
XLA Modules:
  0.0 38.9 jit_solution(12497576349213680238)
XLA Ops:
  0.0 3.6 %own_run.1 = bf16[4,8,24,256]{3,2,1,0:T(8,128)(2,1)} custom-call(bf16[96,2048]{1,0:T(8,128)(2,1)} %constant.2.clone.twiddle_ref, bf16[1,256,2048]{2,1,0:T(8,128)(2,1)} %traces_ref.1, s32[1,1024]{1,0:T(1,128)} %bitcast.3, s32[1,1024]{1,0:T(1,128)} %offset_ref.1), custom_call_target="tpu_custom_call" | custom-call | tf_op jit(solution)/shard_map/own_run/pallas_call | solution.py:329
  3.6 21.0 %all_to_all.5.lists_ref = bf16[32,24,256]{2,1,0:T(8,128)(2,1)} all-to-all(bf16[32,24,256]{2,1,0:T(8,128)(2,1)} %bitcast.2), channel_id=1, replica_groups=mesh['band'=4,'tile'=8] {'band','tile'}, dimensions={0} | all-to-all | bytes 786432 | tf_op jit(solution)/shard_map/all_to_all | solution.py:347
  24.6 14.3 %grid.1 = f32[10,2,64,512]{3,2,1,0:T(8,128)} custom-call(bf16[32,24,256]{2,1,0:T(8,128)(2,1)} %all_to_all.5.lists_ref), custom_call_target="tpu_custom_call" | custom-call | tf_op jit(solution)/shard_map/grid/pallas_call | solution.py:369

commit v12 on v10

--- a/solution.py
+++ b/solution.py
@@ -21,8 +21,9 @@
 COPY = 32
 WIDTHS = (256, 512, 640)
 LARGE = WIDTHS[-1]
-BESIDE = 2
+BESIDE = 5
 SIDE = 4
+TURN = 128
 HALF = 256
 VMEM = 56 * 1024 * 1024
 
@@ -146,7 +147,7 @@
     return pl.ds(pl.multiple_of(b * BLOCK, BLOCK), BLOCK)
 
 
-def add_blocks(table_s, flat, buffers, now, later, packed, total, emit):
+def add_blocks(table_s, flat, buffers, later, packed, total, emit):
     sides = BLOCKS // SIDE
 
     def merge(i, q):
@@ -156,10 +157,11 @@
         later[q] = turned(0, LARGE, buffers[q])
 
     def fast(i, width):
+        parts = [later[q, :, :width] for q in range(SIDE)]
         for q in range(SIDE):
             merge(i + 1, q)
             b = i * SIDE + q
-            for lanes, sums in products(now[q, :, :width], table_s[2 * GROUP + 1, b]):
+            for lanes, sums in products(parts[q], table_s[2 * GROUP + 1, b]):
                 emit(b, lanes, sums)
 
     def slow(b):
@@ -196,7 +198,6 @@
         for q in range(1, SIDE):
             widest = jnp.maximum(widest, table_s[2 * GROUP, b + q])
             largest = jnp.maximum(largest, table_s[2 * GROUP + 1, b + q])
-        now[...] = later[...]
         plain = widest <= COPY
         least = -1
         for width in WIDTHS:
@@ -226,8 +227,8 @@
 ):
     runs = lists_ref.shape[0]
     alone = runs == GROUP
-    now, later, *buffers = rest[: SIDE + 2]
-    grid = rest[SIDE + 2] if not alone else None
+    later, *buffers = rest[: SIDE + 1]
+    grid = rest[SIDE + 1] if not alone else None
 
     def finish(sums, rows, lanes):
         inverse = 1.0 / jnp.maximum(sums(0), 1.0)
@@ -246,7 +247,7 @@
         copy = make_table(g * GROUP, lists_ref, keys, table, table_s, sem)
         turn_runs(g * GROUP, lists_ref, flat)
         copy.wait()
-        add_blocks(table_s, flat, buffers, now, later, packed, total, emit)
+        add_blocks(table_s, flat, buffers, later, packed, total, emit)
         return 0
 
     if alone:
@@ -262,26 +263,35 @@
 
         lax.fori_loop(0, BLOCKS, divide, 0)
 
-    own_rows = pl.ds(pl.multiple_of(lax.axis_index("tile") * row_block, row_block), row_block)
+    first_row = pl.multiple_of(lax.axis_index("tile") * row_block, row_block)
 
     def sent(f):
         return pltpu.make_async_copy(result.at[f], out_ref.at[f], out_sems.at[f])
 
     def frequency(f, slot):
         for part, p in enumerate((f, FB + f)):
-            plane = planes[p]
-            twice[slot + part] = plane + jnp.transpose(plane)
-        own = jnp.concatenate([twice[slot, own_rows, :], twice[slot + 1, own_rows, :]], axis=0)
-        by_real = jnp.dot(own, twice[slot], preferred_element_type=jnp.float32)
-        by_imag = jnp.dot(own, twice[slot + 1], preferred_element_type=jnp.float32)
-        quarter = 0.25 * scale
-        result[f, 0] = (by_real[:row_block] - by_imag[row_block:]) * quarter
-        result[f, 1] = (by_imag[:row_block] + by_real[row_block:]) * quarter
+            for i in range(0, NG, TURN):
+                for j in range(0, NG, TURN):
+                    across = jnp.transpose(planes[p, j : j + TURN, i : i + TURN])
+                    twice[slot, part * NG + i : part * NG + i + TURN, j : j + TURN] = (
+                        planes[p, i : i + TURN, j : j + TURN] + across
+                    )
+        real = twice[slot, pl.ds(first_row, row_block), :]
+        imag = twice[slot, pl.ds(NG + first_row, row_block), :]
+        own = jnp.concatenate(
+            [jnp.concatenate([real, -imag], axis=1), jnp.concatenate([imag, real], axis=1)], axis=0
+        )
+        for half in range(NG // HALF):
+            lanes = slice(half * HALF, (half + 1) * HALF)
+            both = jnp.dot(own, twice[slot, :, lanes], preferred_element_type=jnp.float32)
+            both = both * (0.25 * scale)
+            result[f, 0, :, lanes] = both[:row_block]
+            result[f, 1, :, lanes] = both[row_block:]
         sent(f).start()
 
     def some(i, _):
         for q in range(BESIDE):
-            frequency(i * BESIDE + q, 2 * q)
+            frequency(i * BESIDE + q, q)
         return 0
 
     lax.fori_loop(0, FB // BESIDE, some, 0)
@@ -327,14 +337,14 @@
         pltpu.VMEM((traces + LARGE, 128), jnp.float32),
         pltpu.VMEM((GROUP, 128), jnp.float32),
         pltpu.VMEM((2 * GROUP + 8, 128), jnp.int32),
-        pltpu.VMEM((2 * BESIDE, NG, NG), jnp.bfloat16),
+        pltpu.VMEM((BESIDE, 2 * NG, NG), jnp.bfloat16),
         pltpu.VMEM(((CH + 1) * BLOCK, NG), jnp.float32),
         pltpu.VMEM((FB, 2, row_block, NG), jnp.float32),
         pltpu.SMEM((2 * GROUP + 8, 128), jnp.int32),
         pltpu.SemaphoreType.DMA,
         pltpu.SemaphoreType.DMA((FB,)),
     ]
-    scratch += [pltpu.VMEM((SIDE, ROWS, LARGE), jnp.float32)] * 2
+    scratch.append(pltpu.VMEM((SIDE, ROWS, LARGE), jnp.float32))
     scratch += [pltpu.VMEM((LARGE + COPY, 128), jnp.float32)] * SIDE
     if runs != GROUP:
         scratch.append(pltpu.VMEM((CH + 1, NG, NG), jnp.float32))

time: 39.2 us -> 38.3 us (0.977)
  Pallas kernels: 18.2 us -> 17.1 us
    pallas_call x1, Pallas kernels: 15.4 us -> 14.4 us  [per_device(): pl.pallas_call(functools.partial(grid_kernel, 1.0 / math.sqrt(NG), row_bl...]
where the time goes in v12:
time: 38.3 us; the launch traced here: 38.1 us
  blocking collectives  21 us (55%)
  Pallas kernels  17.1 us (45%)
    all_to_all x1, blocking collectives, per_device(): lax.all_to_all(own.reshape(runs, ROWS, count), ('band', 'tile'), split_ax...  21 us
    pallas_call x1, Pallas kernels, per_device(): pl.pallas_call(functools.partial(grid_kernel, 1.0 / math.sqrt(NG), row_bl...  14.4 us
    pallas_call x1, Pallas kernels, per_device(): pl.pallas_call(functools.partial(run_kernel, cells_dev), out_shape=jax.Sh...  2.71 us

profile of v12, /device:TPU:0, one launch (start us, length us, event | category | flops | bytes accessed | tf_op | source)
XLA Modules:
  0.0 38.1 jit_solution(4068538306779223840)
XLA Ops:
  0.0 2.7 %own_run.1 = bf16[4,8,24,256]{3,2,1,0:T(8,128)(2,1)} custom-call(bf16[96,2048]{1,0:T(8,128)(2,1)} %constant.2.clone.twiddle_ref, bf16[1,256,2048]{2,1,0:T(8,128)(2,1)} %traces_ref.1, s32[1,1024]{1,0:T(1,128)} %bitcast.3, s32[1,1024]{1,0:T(1,128)} %offset_ref.1), custom_call_target="tpu_custom_call" | custom-call | tf_op jit(solution)/shard_map/own_run/pallas_call | solution.py:316
  2.7 21.0 %all_to_all.5.lists_ref = bf16[32,24,256]{2,1,0:T(8,128)(2,1)} all-to-all(bf16[32,24,256]{2,1,0:T(8,128)(2,1)} %bitcast.2), channel_id=1, replica_groups=mesh['band'=4,'tile'=8] {'band','tile'}, dimensions={0} | all-to-all | bytes 786432 | tf_op jit(solution)/shard_map/all_to_all | solution.py:329
  23.7 14.4 %grid.1 = f32[10,2,64,512]{3,2,1,0:T(8,128)} custom-call(bf16[32,24,256]{2,1,0:T(8,128)(2,1)} %all_to_all.5.lists_ref), custom_call_target="tpu_custom_call" | custom-call | tf_op jit(solution)/shard_map/grid/pallas_call | solution.py:351

commit v13 on v12

--- a/solution.py
+++ b/solution.py
@@ -15,6 +15,7 @@
 FB = 10
 CH = 2 * FB
 ROWS = 24
+LANES = 32
 BLOCK = 16
 BLOCKS = NG // BLOCK
 GROUP = 32
@@ -22,7 +23,7 @@
 WIDTHS = (256, 512, 640)
 LARGE = WIDTHS[-1]
 BESIDE = 5
-SIDE = 4
+SIDE = 128 // LANES
 TURN = 128
 HALF = 256
 VMEM = 56 * 1024 * 1024
@@ -106,17 +107,18 @@
 
 def turn_runs(first_run, lists_ref, flat):
     length = lists_ref.shape[2]
+    rest = jnp.zeros((LANES - ROWS, length), jnp.float32)
     for r in range(GROUP):
         part = lists_ref[first_run + r].astype(jnp.float32)
+        part = jnp.concatenate([part, rest] * SIDE, axis=0)
         for first in range(0, length, 128):
             at = r * length + first
-            flat[at : at + 128, :ROWS] = jnp.transpose(part[:, first : first + 128])
-
-
-def turned(first, width, packed):
+            flat[at : at + 128, :] = jnp.transpose(part[:, first : first + 128])
+
+
+def turned(first, packed):
     return jnp.concatenate(
-        [jnp.transpose(packed[pl.ds(first + k, 128), :])[:ROWS] for k in range(0, width, 128)],
-        axis=1,
+        [jnp.transpose(packed[pl.ds(first + k, 128), :]) for k in range(0, LARGE, 128)], axis=1
     )
 
 
@@ -147,22 +149,29 @@
     return pl.ds(pl.multiple_of(b * BLOCK, BLOCK), BLOCK)
 
 
-def add_blocks(table_s, flat, buffers, later, packed, total, emit):
+def add_blocks(table_s, flat, buffer, later, packed, total, emit):
     sides = BLOCKS // SIDE
+
+    lane = lax.broadcasted_iota(jnp.int32, (COPY, 128), 1)
 
     def merge(i, q):
         b = jnp.minimum(i, sides - 1) * SIDE + q
+        mine = (lane >= q * LANES) & (lane < (q + 1) * LANES)
         for r in range(GROUP):
-            buffers[q][pl.ds(table_s[GROUP + r, b], COPY), :] = flat[pl.ds(table_s[r, b], COPY), :]
-        later[q] = turned(0, LARGE, buffers[q])
+            pltpu.store(
+                buffer.at[pl.ds(table_s[GROUP + r, b], COPY), :],
+                flat[pl.ds(table_s[r, b], COPY), :],
+                mask=mine,
+            )
 
     def fast(i, width):
-        parts = [later[q, :, :width] for q in range(SIDE)]
+        parts = [later[q * LANES : q * LANES + ROWS, :width] for q in range(SIDE)]
         for q in range(SIDE):
             merge(i + 1, q)
             b = i * SIDE + q
             for lanes, sums in products(parts[q], table_s[2 * GROUP + 1, b]):
                 emit(b, lanes, sums)
+        later[...] = turned(0, buffer)
 
     def slow(b):
         def run(r, target):
@@ -182,7 +191,7 @@
 
         def piece(k, _):
             first = pl.multiple_of(k * LARGE, LARGE)
-            for lanes, sums in products(turned(first, LARGE, packed), size - first):
+            for lanes, sums in products(turned(first, packed)[:ROWS], size - first):
                 total[:, lanes] += sums
             return 0
 
@@ -212,12 +221,14 @@
         def _():
             for q in range(SIDE):
                 merge(i + 1, q)
+            later[...] = turned(0, buffer)
             lax.fori_loop(0, SIDE, lambda q, _: (slow(b + q), 0)[1], 0)
 
         return 0
 
     for q in range(SIDE):
         merge(jnp.int32(0), q)
+    later[...] = turned(0, buffer)
     lax.fori_loop(0, sides, side, 0)
 
 
@@ -227,8 +238,8 @@
 ):
     runs = lists_ref.shape[0]
     alone = runs == GROUP
-    later, *buffers = rest[: SIDE + 1]
-    grid = rest[SIDE + 1] if not alone else None
+    later, buffer = rest[:2]
+    grid = rest[2] if not alone else None
 
     def finish(sums, rows, lanes):
         inverse = 1.0 / jnp.maximum(sums(0), 1.0)
@@ -247,7 +258,7 @@
         copy = make_table(g * GROUP, lists_ref, keys, table, table_s, sem)
         turn_runs(g * GROUP, lists_ref, flat)
         copy.wait()
-        add_blocks(table_s, flat, buffers, later, packed, total, emit)
+        add_blocks(table_s, flat, buffer, later, packed, total, emit)
         return 0
 
     if alone:
@@ -344,8 +355,8 @@
         pltpu.SemaphoreType.DMA,
         pltpu.SemaphoreType.DMA((FB,)),
     ]
-    scratch.append(pltpu.VMEM((SIDE, ROWS, LARGE), jnp.float32))
-    scratch += [pltpu.VMEM((LARGE + COPY, 128), jnp.float32)] * SIDE
+    scratch.append(pltpu.VMEM((128, LARGE), jnp.float32))
+    scratch.append(pltpu.VMEM((LARGE + COPY, 128), jnp.float32))
     if runs != GROUP:
         scratch.append(pltpu.VMEM((CH + 1, NG, NG), jnp.float32))
     return pl.pallas_call(

time: 38.3 us -> 39.1 us (1.021)
  Pallas kernels: 17.1 us -> 17.9 us
    pallas_call x1, Pallas kernels: 14.4 us -> 15.2 us  [per_device(): pl.pallas_call(functools.partial(grid_kernel, 1.0 / math.sqrt(NG), row_bl...]
where the time goes in v13:
time: 39.1 us; the launch traced here: 38.9 us
  blocking collectives  21 us (54%)
  Pallas kernels  17.9 us (46%)
    all_to_all x1, blocking collectives, per_device(): lax.all_to_all(own.reshape(runs, ROWS, count), ('band', 'tile'), split_ax...  21 us
    pallas_call x1, Pallas kernels, per_device(): pl.pallas_call(functools.partial(grid_kernel, 1.0 / math.sqrt(NG), row_bl...  15.2 us
    pallas_call x1, Pallas kernels, per_device(): pl.pallas_call(functools.partial(run_kernel, cells_dev), out_shape=jax.Sh...  2.71 us

profile of v13, /device:TPU:0, one launch (start us, length us, event | category | flops | bytes accessed | tf_op | source)
XLA Modules:
  0.0 38.9 jit_solution(874625395111709667)
XLA Ops:
  0.0 2.7 %own_run.1 = bf16[4,8,24,256]{3,2,1,0:T(8,128)(2,1)} custom-call(bf16[96,2048]{1,0:T(8,128)(2,1)} %constant.2.clone.twiddle_ref, bf16[1,256,2048]{2,1,0:T(8,128)(2,1)} %traces_ref.1, s32[1,1024]{1,0:T(1,128)} %bitcast.3, s32[1,1024]{1,0:T(1,128)} %offset_ref.1), custom_call_target="tpu_custom_call" | custom-call | tf_op jit(solution)/shard_map/own_run/pallas_call | solution.py:327
  2.7 21.0 %all_to_all.5.lists_ref = bf16[32,24,256]{2,1,0:T(8,128)(2,1)} all-to-all(bf16[32,24,256]{2,1,0:T(8,128)(2,1)} %bitcast.2), channel_id=1, replica_groups=mesh['band'=4,'tile'=8] {'band','tile'}, dimensions={0} | all-to-all | bytes 786432 | tf_op jit(solution)/shard_map/all_to_all | solution.py:340
  23.7 15.2 %grid.1 = f32[10,2,64,512]{3,2,1,0:T(8,128)} custom-call(bf16[32,24,256]{2,1,0:T(8,128)(2,1)} %all_to_all.5.lists_ref), custom_call_target="tpu_custom_call" | custom-call | tf_op jit(solution)/shard_map/grid/pallas_call | solution.py:362

commit v14 on v12

--- a/solution.py
+++ b/solution.py
@@ -15,8 +15,10 @@
 FB = 10
 CH = 2 * FB
 ROWS = 24
-BLOCK = 16
-BLOCKS = NG // BLOCK
+BLOCK = 32
+HALF = 256
+HALVES = NG // HALF
+BLOCKS = NG // BLOCK * HALVES
 GROUP = 32
 COPY = 32
 WIDTHS = (256, 512, 640)
@@ -24,7 +26,6 @@
 BESIDE = 5
 SIDE = 4
 TURN = 128
-HALF = 256
 VMEM = 56 * 1024 * 1024
 
 
@@ -49,11 +50,13 @@
     bands, tiles, _, count = out_ref.shape
     lanes = pl.ds(pl.multiple_of(lax.axis_index("band") * count, count), count)
     cell = owner_ref[:, lanes] * cells_dev + offset_ref[:, lanes]
-    order = cell * count + lax.broadcasted_iota(jnp.int32, (1, count), 1)
+    source = cell // NG
+    receiver = cell % NG
+    block = source // BLOCK * HALVES + receiver // HALF
+    order = block * count + lax.broadcasted_iota(jnp.int32, (1, count), 1)
     rank = jnp.zeros((1, count), jnp.int32)
     starts = jnp.zeros((1, count), jnp.int32)
-    limit = lax.broadcasted_iota(jnp.int32, (1, count), 1) * (BLOCK * NG * count)
-    limit = jnp.minimum(limit, NG * NG * count)
+    limit = lax.broadcasted_iota(jnp.int32, (1, count), 1) * count
     for first in range(0, count, 128):
         column = jnp.transpose(jnp.broadcast_to(order[:, first : first + 128], (128, 128)))
         column = jnp.concatenate([column] * (count // 128), axis=1)
@@ -61,12 +64,9 @@
         starts += jnp.sum((column < limit).astype(jnp.int32), axis=0, keepdims=True)
     target = lax.broadcasted_iota(jnp.int32, (count, count), 0)
     permute = (target == rank).astype(jnp.float32).astype(jnp.bfloat16)
-    source = cell // NG
-    receiver = cell % NG
     row = lax.broadcasted_iota(jnp.int32, (bands * ROWS, count), 0) % ROWS
     digits = jnp.where(row == CH + 1, source % BLOCK, 0)
-    digits = jnp.where(row == CH + 2, receiver // HALF, digits)
-    digits = jnp.where(row == CH + 3, receiver % HALF, digits)
+    digits = jnp.where(row == CH + 2, receiver % HALF, digits)
     spectra = contract_last(twiddle_ref[...], traces_ref[0])
     packed = (spectra + digits.astype(jnp.float32)).astype(jnp.bfloat16)
     ordered = contract_last(packed, permute) + jnp.where(row == CH, starts, 0).astype(jnp.float32)
@@ -134,17 +134,14 @@
     hit = spread(jnp.where(place < size, part[CH + 1 : CH + 2], -1.0)) == step
     left = [jnp.where(hit, one, none)]
     left += [jnp.where(hit, spread(part[c : c + 1]), none) for c in range(CH)]
-    left = jnp.concatenate(left, axis=0)
-    for half in range(NG // HALF):
-        low = spread(jnp.where(part[CH + 2 : CH + 3] == float(half), part[CH + 3 : CH + 4], -1.0))
-        right = [
-            jnp.where(low == step + jnp.bfloat16(j), one, none) for j in range(0, HALF, BLOCK)
-        ]
-        yield pl.ds(half * HALF, HALF), contract_last(left, jnp.concatenate(right, axis=0))
-
-
-def block_rows(b):
-    return pl.ds(pl.multiple_of(b * BLOCK, BLOCK), BLOCK)
+    receiver = spread(part[CH + 2 : CH + 3])
+    right = [jnp.where(receiver == step + jnp.bfloat16(j), one, none) for j in range(0, HALF, BLOCK)]
+    return contract_last(jnp.concatenate(left, axis=0), jnp.concatenate(right, axis=0))
+
+
+def spot(b):
+    rows = pl.ds(pl.multiple_of(b // HALVES * BLOCK, BLOCK), BLOCK)
+    return rows, pl.ds(pl.multiple_of(b % HALVES * HALF, HALF), HALF)
 
 
 def add_blocks(table_s, flat, buffers, later, packed, total, emit):
@@ -161,8 +158,7 @@
         for q in range(SIDE):
             merge(i + 1, q)
             b = i * SIDE + q
-            for lanes, sums in products(parts[q], table_s[2 * GROUP + 1, b]):
-                emit(b, lanes, sums)
+            emit(b, products(parts[q], table_s[2 * GROUP + 1, b]))
 
     def slow(b):
         def run(r, target):
@@ -182,14 +178,11 @@
 
         def piece(k, _):
             first = pl.multiple_of(k * LARGE, LARGE)
-            for lanes, sums in products(turned(first, LARGE, packed), size - first):
-                total[:, lanes] += sums
+            total[...] += products(turned(first, LARGE, packed), size - first)
             return 0
 
         lax.fori_loop(0, (size + LARGE - 1) // LARGE, piece, 0)
-        for half in range(NG // HALF):
-            lanes = pl.ds(half * HALF, HALF)
-            emit(b, lanes, total[:, lanes])
+        emit(b, total[...])
 
     def side(i, _):
         b = i * SIDE
@@ -235,8 +228,8 @@
         for c in range(CH):
             planes[c, rows, lanes] = (sums(c + 1) * inverse).astype(jnp.bfloat16)
 
-    def emit(b, lanes, sums):
-        rows = block_rows(b)
+    def emit(b, sums):
+        rows, lanes = spot(b)
         if alone:
             finish(lambda c: sums[c * BLOCK : (c + 1) * BLOCK], rows, lanes)
         else:
@@ -257,8 +250,8 @@
         lax.fori_loop(0, runs // GROUP, group, 0)
 
         def divide(b, _):
-            rows = block_rows(b)
-            finish(lambda c: grid[c, rows, :], rows, pl.ds(0, NG))
+            rows, lanes = spot(b)
+            finish(lambda c: grid[c, rows, lanes], rows, lanes)
             return 0
 
         lax.fori_loop(0, BLOCKS, divide, 0)
@@ -338,7 +331,7 @@
         pltpu.VMEM((GROUP, 128), jnp.float32),
         pltpu.VMEM((2 * GROUP + 8, 128), jnp.int32),
         pltpu.VMEM((BESIDE, 2 * NG, NG), jnp.bfloat16),
-        pltpu.VMEM(((CH + 1) * BLOCK, NG), jnp.float32),
+        pltpu.VMEM(((CH + 1) * BLOCK, HALF), jnp.float32),
         pltpu.VMEM((FB, 2, row_block, NG), jnp.float32),
         pltpu.SMEM((2 * GROUP + 8, 128), jnp.int32),
         pltpu.SemaphoreType.DMA,

time: 38.3 us -> 39.3 us (1.026)
  Pallas kernels: 17.1 us -> 17.9 us
    pallas_call x1, Pallas kernels: 14.4 us -> 15.2 us  [per_device(): pl.pallas_call(functools.partial(grid_kernel, 1.0 / math.sqrt(NG), row_bl...]
where the time goes in v14:
time: 39.3 us; the launch traced here: 38.9 us
  blocking collectives  21 us (53%)
  Pallas kernels  17.9 us (46%)
    all_to_all x1, blocking collectives, per_device(): lax.all_to_all(own.reshape(runs, ROWS, count), ('band', 'tile'), split_ax...  21 us
    pallas_call x1, Pallas kernels, per_device(): pl.pallas_call(functools.partial(grid_kernel, 1.0 / math.sqrt(NG), row_bl...  15.2 us
    pallas_call x1, Pallas kernels, per_device(): pl.pallas_call(functools.partial(run_kernel, cells_dev), out_shape=jax.Sh...  2.72 us

profile of v14, /device:TPU:0, one launch (start us, length us, event | category | flops | bytes accessed | tf_op | source)
XLA Modules:
  0.0 38.9 jit_solution(16281043113474075078)
XLA Ops:
  0.0 2.7 %own_run.1 = bf16[4,8,24,256]{3,2,1,0:T(8,128)(2,1)} custom-call(bf16[96,2048]{1,0:T(8,128)(2,1)} %constant.2.clone.twiddle_ref, bf16[1,256,2048]{2,1,0:T(8,128)(2,1)} %traces_ref.1, s32[1,1024]{1,0:T(1,128)} %bitcast.3, s32[1,1024]{1,0:T(1,128)} %offset_ref.1), custom_call_target="tpu_custom_call" | custom-call | tf_op jit(solution)/shard_map/own_run/pallas_call | solution.py:309
  2.7 21.0 %all_to_all.5.lists_ref = bf16[32,24,256]{2,1,0:T(8,128)(2,1)} all-to-all(bf16[32,24,256]{2,1,0:T(8,128)(2,1)} %bitcast.2), channel_id=1, replica_groups=mesh['band'=4,'tile'=8] {'band','tile'}, dimensions={0} | all-to-all | bytes 786432 | tf_op jit(solution)/shard_map/all_to_all | solution.py:322
  23.7 15.2 %grid.1 = f32[10,2,64,512]{3,2,1,0:T(8,128)} custom-call(bf16[32,24,256]{2,1,0:T(8,128)(2,1)} %all_to_all.5.lists_ref), custom_call_target="tpu_custom_call" | custom-call | tf_op jit(solution)/shard_map/grid/pallas_call | solution.py:344

commit v15 on v12

--- a/solution.py
+++ b/solution.py
@@ -19,7 +19,7 @@
 BLOCKS = NG // BLOCK
 GROUP = 32
 COPY = 32
-WIDTHS = (256, 512, 640)
+WIDTHS = (128, 256, 384, 512, 640)
 LARGE = WIDTHS[-1]
 BESIDE = 5
 SIDE = 4

time: 38.3 us -> 38.5 us (level)
  Pallas kernels: 17.1 us -> 17.6 us
    pallas_call x1, Pallas kernels: 14.4 us -> 14.9 us  [per_device(): pl.pallas_call(functools.partial(grid_kernel, 1.0 / math.sqrt(NG), row_bl...]
where the time goes in v15:
time: 38.5 us
  blocking collectives  21 us (55%)
  Pallas kernels  17.6 us (46%)
    all_to_all x1, blocking collectives, per_device(): lax.all_to_all(own.reshape(runs, ROWS, count), ('band', 'tile'), split_ax...  21 us
    pallas_call x1, Pallas kernels, per_device(): pl.pallas_call(functools.partial(grid_kernel, 1.0 / math.sqrt(NG), row_bl...  14.9 us
    pallas_call x1, Pallas kernels, per_device(): pl.pallas_call(functools.partial(run_kernel, cells_dev), out_shape=jax.Sh...  2.71 us

profile of v15, /device:TPU:0, one launch (start us, length us, event | category | flops | bytes accessed | tf_op | source)
XLA Modules:
  0.0 38.5 jit_solution(11946996668615009368)
XLA Ops:
  0.0 2.7 %own_run.1 = bf16[4,8,24,256]{3,2,1,0:T(8,128)(2,1)} custom-call(bf16[96,2048]{1,0:T(8,128)(2,1)} %constant.2.clone.twiddle_ref, bf16[1,256,2048]{2,1,0:T(8,128)(2,1)} %traces_ref.1, s32[1,1024]{1,0:T(1,128)} %bitcast.3, s32[1,1024]{1,0:T(1,128)} %offset_ref.1), custom_call_target="tpu_custom_call" | custom-call | tf_op jit(solution)/shard_map/own_run/pallas_call | solution.py:316
  2.7 21.0 %all_to_all.5.lists_ref = bf16[32,24,256]{2,1,0:T(8,128)(2,1)} all-to-all(bf16[32,24,256]{2,1,0:T(8,128)(2,1)} %bitcast.2), channel_id=1, replica_groups=mesh['band'=4,'tile'=8] {'band','tile'}, dimensions={0} | all-to-all | bytes 786432 | tf_op jit(solution)/shard_map/all_to_all | solution.py:329
  23.7 14.9 %grid.1 = f32[10,2,64,512]{3,2,1,0:T(8,128)} custom-call(bf16[32,24,256]{2,1,0:T(8,128)(2,1)} %all_to_all.5.lists_ref), custom_call_target="tpu_custom_call" | custom-call | tf_op jit(solution)/shard_map/grid/pallas_call | solution.py:351

commit v16 on v12

--- a/solution.py
+++ b/solution.py
@@ -46,7 +46,7 @@
 
 
 def run_kernel(cells_dev, twiddle_ref, traces_ref, owner_ref, offset_ref, out_ref):
-    bands, tiles, _, count = out_ref.shape
+    tiles, bands, _, count = out_ref.shape
     lanes = pl.ds(pl.multiple_of(lax.axis_index("band") * count, count), count)
     cell = owner_ref[:, lanes] * cells_dev + offset_ref[:, lanes]
     order = cell * count + lax.broadcasted_iota(jnp.int32, (1, count), 1)
@@ -73,7 +73,7 @@
     for band in range(bands):
         part = ordered[band * ROWS : (band + 1) * ROWS].astype(jnp.bfloat16)
         for tile in range(tiles):
-            out_ref[band, tile] = part
+            out_ref[tile, band] = part
 
 
 def make_table(first_run, lists_ref, keys, table, table_s, sem):
@@ -315,7 +315,7 @@
 
     own = pl.pallas_call(
         functools.partial(run_kernel, cells_dev),
-        out_shape=jax.ShapeDtypeStruct((band_count, tile_count, ROWS, count), jnp.bfloat16),
+        out_shape=jax.ShapeDtypeStruct((tile_count, band_count, ROWS, count), jnp.bfloat16),
         in_specs=[whole()] * 4,
         out_specs=whole(),
         compiler_params=params,
@@ -327,7 +327,7 @@
         bin_offset,
     )
     lists = lax.all_to_all(
-        own.reshape(runs, ROWS, count), ("band", "tile"), split_axis=0, concat_axis=0, tiled=True
+        own.reshape(runs, ROWS, count), ("tile", "band"), split_axis=0, concat_axis=0, tiled=True
     )
 
     traces = GROUP * count

time: 38.3 us -> 37.9 us (0.990)
  blocking collectives: 21 us -> 20.6 us
where the time goes in v16:
time: 37.9 us; the launch traced here: 37.7 us
  blocking collectives  20.6 us (54%)
  Pallas kernels  17.1 us (45%)
    all_to_all x1, blocking collectives, per_device(): lax.all_to_all(own.reshape(runs, ROWS, count), ('tile', 'band'), split_ax...  20.6 us
    pallas_call x1, Pallas kernels, per_device(): pl.pallas_call(functools.partial(grid_kernel, 1.0 / math.sqrt(NG), row_bl...  14.4 us
    pallas_call x1, Pallas kernels, per_device(): pl.pallas_call(functools.partial(run_kernel, cells_dev), out_shape=jax.Sh...  2.71 us

profile of v16, /device:TPU:0, one launch (start us, length us, event | category | flops | bytes accessed | tf_op | source)
XLA Modules:
  0.0 37.7 jit_solution(8863656394025747917)
XLA Ops:
  0.0 2.7 %own_run.1 = bf16[8,4,24,256]{3,2,1,0:T(8,128)(2,1)} custom-call(bf16[96,2048]{1,0:T(8,128)(2,1)} %constant.2.clone.twiddle_ref, bf16[1,256,2048]{2,1,0:T(8,128)(2,1)} %traces_ref.1, s32[1,1024]{1,0:T(1,128)} %bitcast.3, s32[1,1024]{1,0:T(1,128)} %offset_ref.1), custom_call_target="tpu_custom_call" | custom-call | tf_op jit(solution)/shard_map/own_run/pallas_call | solution.py:316
  2.7 20.6 %all_to_all.5.lists_ref = bf16[32,24,256]{2,1,0:T(8,128)(2,1)} all-to-all(bf16[32,24,256]{2,1,0:T(8,128)(2,1)} %bitcast.2), channel_id=1, replica_groups=mesh['band'=4,'tile'=8] {'tile','band'}, dimensions={0} | all-to-all | bytes 786432 | tf_op jit(solution)/shard_map/all_to_all | solution.py:329
  23.3 14.4 %grid.1 = f32[10,2,64,512]{3,2,1,0:T(8,128)} custom-call(bf16[32,24,256]{2,1,0:T(8,128)(2,1)} %all_to_all.5.lists_ref), custom_call_target="tpu_custom_call" | custom-call | tf_op jit(solution)/shard_map/grid/pallas_call | solution.py:351

commit v17 on v16

--- a/solution.py
+++ b/solution.py
@@ -19,6 +19,7 @@
 BLOCKS = NG // BLOCK
 GROUP = 32
 COPY = 32
+NARROW = 16
 WIDTHS = (256, 512, 640)
 LARGE = WIDTHS[-1]
 BESIDE = 5
@@ -150,16 +151,23 @@
 def add_blocks(table_s, flat, buffers, later, packed, total, emit):
     sides = BLOCKS // SIDE
 
-    def merge(i, q):
+    def merge(i, q, rows):
         b = jnp.minimum(i, sides - 1) * SIDE + q
         for r in range(GROUP):
-            buffers[q][pl.ds(table_s[GROUP + r, b], COPY), :] = flat[pl.ds(table_s[r, b], COPY), :]
+            buffers[q][pl.ds(table_s[GROUP + r, b], rows), :] = flat[pl.ds(table_s[r, b], rows), :]
         later[q] = turned(0, LARGE, buffers[q])
 
-    def fast(i, width):
+    def most(i, row):
+        b = jnp.minimum(i, sides - 1) * SIDE
+        found = table_s[row, b]
+        for q in range(1, SIDE):
+            found = jnp.maximum(found, table_s[row, b + q])
+        return found
+
+    def fast(i, width, rows):
         parts = [later[q, :, :width] for q in range(SIDE)]
         for q in range(SIDE):
-            merge(i + 1, q)
+            merge(i + 1, q, rows)
             b = i * SIDE + q
             for lanes, sums in products(parts[q], table_s[2 * GROUP + 1, b]):
                 emit(b, lanes, sums)
@@ -192,32 +200,29 @@
             emit(b, lanes, total[:, lanes])
 
     def side(i, _):
-        b = i * SIDE
-        widest = table_s[2 * GROUP, b]
-        largest = table_s[2 * GROUP + 1, b]
-        for q in range(1, SIDE):
-            widest = jnp.maximum(widest, table_s[2 * GROUP, b + q])
-            largest = jnp.maximum(largest, table_s[2 * GROUP + 1, b + q])
-        plain = widest <= COPY
+        largest = most(i, 2 * GROUP + 1)
+        plain = (most(i, 2 * GROUP) <= COPY) & (largest <= LARGE)
+        ahead = most(i + 1, 2 * GROUP) <= NARROW
         least = -1
         for width in WIDTHS:
-
-            @pl.when(plain & (largest > least) & (largest <= width))
-            def _(width=width):
-                fast(i, width)
+            for rows, fits in ((NARROW, ahead), (COPY, jnp.logical_not(ahead))):
+
+                @pl.when(plain & (largest > least) & (largest <= width) & fits)
+                def _(width=width, rows=rows):
+                    fast(i, width, rows)
 
             least = width
 
-        @pl.when(jnp.logical_not(plain) | (largest > LARGE))
+        @pl.when(jnp.logical_not(plain))
         def _():
             for q in range(SIDE):
-                merge(i + 1, q)
-            lax.fori_loop(0, SIDE, lambda q, _: (slow(b + q), 0)[1], 0)
+                merge(i + 1, q, COPY)
+            lax.fori_loop(0, SIDE, lambda q, _: (slow(i * SIDE + q), 0)[1], 0)
 
         return 0
 
     for q in range(SIDE):
-        merge(jnp.int32(0), q)
+        merge(jnp.int32(0), q, COPY)
     lax.fori_loop(0, sides, side, 0)
 
 

time: 37.9 us -> 38.3 us (1.011)
  Pallas kernels: 17.1 us -> 17.7 us
    pallas_call x1, Pallas kernels: 14.4 us -> 15 us  [per_device(): pl.pallas_call(functools.partial(grid_kernel, 1.0 / math.sqrt(NG), row_bl...]
where the time goes in v17:
time: 38.3 us
  blocking collectives  20.6 us (54%)
  Pallas kernels  17.7 us (46%)
    all_to_all x1, blocking collectives, per_device(): lax.all_to_all(own.reshape(runs, ROWS, count), ('tile', 'band'), split_ax...  20.6 us
    pallas_call x1, Pallas kernels, per_device(): pl.pallas_call(functools.partial(grid_kernel, 1.0 / math.sqrt(NG), row_bl...  15 us
    pallas_call x1, Pallas kernels, per_device(): pl.pallas_call(functools.partial(run_kernel, cells_dev), out_shape=jax.Sh...  2.71 us

profile of v17, /device:TPU:0, one launch (start us, length us, event | category | flops | bytes accessed | tf_op | source)
XLA Modules:
  0.0 38.3 jit_solution(14545377517618772454)
XLA Ops:
  0.0 2.7 %own_run.1 = bf16[8,4,24,256]{3,2,1,0:T(8,128)(2,1)} custom-call(bf16[96,2048]{1,0:T(8,128)(2,1)} %constant.2.clone.twiddle_ref, bf16[1,256,2048]{2,1,0:T(8,128)(2,1)} %traces_ref.1, s32[1,1024]{1,0:T(1,128)} %bitcast.3, s32[1,1024]{1,0:T(1,128)} %offset_ref.1), custom_call_target="tpu_custom_call" | custom-call | tf_op jit(solution)/shard_map/own_run/pallas_call | solution.py:321
  2.7 20.6 %all_to_all.5.lists_ref = bf16[32,24,256]{2,1,0:T(8,128)(2,1)} all-to-all(bf16[32,24,256]{2,1,0:T(8,128)(2,1)} %bitcast.2), channel_id=1, replica_groups=mesh['band'=4,'tile'=8] {'tile','band'}, dimensions={0} | all-to-all | bytes 786432 | tf_op jit(solution)/shard_map/all_to_all | solution.py:334
  23.3 15.0 %grid.1 = f32[10,2,64,512]{3,2,1,0:T(8,128)} custom-call(bf16[32,24,256]{2,1,0:T(8,128)(2,1)} %all_to_all.5.lists_ref), custom_call_target="tpu_custom_call" | custom-call | tf_op jit(solution)/shard_map/grid/pallas_call | solution.py:356

commit v18 on v16

--- a/solution.py
+++ b/solution.py
@@ -18,10 +18,11 @@
 BLOCK = 16
 BLOCKS = NG // BLOCK
 GROUP = 32
+TURNED = 8
 COPY = 32
 WIDTHS = (256, 512, 640)
 LARGE = WIDTHS[-1]
-BESIDE = 5
+BESIDE = 2
 SIDE = 4
 TURN = 128
 HALF = 256
@@ -106,11 +107,17 @@
 
 def turn_runs(first_run, lists_ref, flat):
     length = lists_ref.shape[2]
-    for r in range(GROUP):
-        part = lists_ref[first_run + r].astype(jnp.float32)
-        for first in range(0, length, 128):
-            at = r * length + first
-            flat[at : at + 128, :ROWS] = jnp.transpose(part[:, first : first + 128])
+
+    def some(i, _):
+        for k in range(TURNED):
+            r = i * TURNED + k
+            part = lists_ref[first_run + r].astype(jnp.float32)
+            for first in range(0, length, 128):
+                at = pl.multiple_of(r * length + first, 128)
+                flat[pl.ds(at, 128), :ROWS] = jnp.transpose(part[:, first : first + 128])
+        return 0
+
+    lax.fori_loop(0, GROUP // TURNED, some, 0)
 
 
 def turned(first, width, packed):

time: 37.9 us -> 38.4 us (1.013)
  Pallas kernels: 17.1 us -> 17.6 us
    pallas_call x1, Pallas kernels: 14.4 us -> 14.9 us  [per_device(): pl.pallas_call(functools.partial(grid_kernel, 1.0 / math.sqrt(NG), row_bl...]
where the time goes in v18:
time: 38.4 us; the launch traced here: 38.2 us
  blocking collectives  20.6 us (54%)
  Pallas kernels  17.6 us (46%)
    all_to_all x1, blocking collectives, per_device(): lax.all_to_all(own.reshape(runs, ROWS, count), ('tile', 'band'), split_ax...  20.6 us
    pallas_call x1, Pallas kernels, per_device(): pl.pallas_call(functools.partial(grid_kernel, 1.0 / math.sqrt(NG), row_bl...  14.9 us
    pallas_call x1, Pallas kernels, per_device(): pl.pallas_call(functools.partial(run_kernel, cells_dev), out_shape=jax.Sh...  2.71 us

profile of v18, /device:TPU:0, one launch (start us, length us, event | category | flops | bytes accessed | tf_op | source)
XLA Modules:
  0.0 38.2 jit_solution(9225751906449832596)
XLA Ops:
  0.0 2.7 %own_run.1 = bf16[8,4,24,256]{3,2,1,0:T(8,128)(2,1)} custom-call(bf16[96,2048]{1,0:T(8,128)(2,1)} %constant.2.clone.twiddle_ref, bf16[1,256,2048]{2,1,0:T(8,128)(2,1)} %traces_ref.1, s32[1,1024]{1,0:T(1,128)} %bitcast.3, s32[1,1024]{1,0:T(1,128)} %offset_ref.1), custom_call_target="tpu_custom_call" | custom-call | tf_op jit(solution)/shard_map/own_run/pallas_call | solution.py:323
  2.7 20.6 %all_to_all.5.lists_ref = bf16[32,24,256]{2,1,0:T(8,128)(2,1)} all-to-all(bf16[32,24,256]{2,1,0:T(8,128)(2,1)} %bitcast.2), channel_id=1, replica_groups=mesh['band'=4,'tile'=8] {'tile','band'}, dimensions={0} | all-to-all | bytes 786432 | tf_op jit(solution)/shard_map/all_to_all | solution.py:336
  23.3 14.9 %grid.1 = f32[10,2,64,512]{3,2,1,0:T(8,128)} custom-call(bf16[32,24,256]{2,1,0:T(8,128)(2,1)} %all_to_all.5.lists_ref), custom_call_target="tpu_custom_call" | custom-call | tf_op jit(solution)/shard_map/grid/pallas_call | solution.py:358

commit v19 on v16

--- a/solution.py
+++ b/solution.py
@@ -120,8 +120,7 @@
     )
 
 
-def products(part, size):
-    width = part.shape[1]
+def products(row_of, width, size):
     step = lax.broadcasted_iota(jnp.int32, (BLOCK, width), 0).astype(jnp.float32)
     step = step.astype(jnp.bfloat16)
     place = lax.broadcasted_iota(jnp.int32, (1, width), 1)
@@ -131,12 +130,13 @@
     def spread(row):
         return jnp.broadcast_to(row, (BLOCK, width)).astype(jnp.bfloat16)
 
-    hit = spread(jnp.where(place < size, part[CH + 1 : CH + 2], -1.0)) == step
+    hit = spread(jnp.where(place < size, row_of(CH + 1), -1.0)) == step
     left = [jnp.where(hit, one, none)]
-    left += [jnp.where(hit, spread(part[c : c + 1]), none) for c in range(CH)]
+    left += [jnp.where(hit, spread(row_of(c)), none) for c in range(CH)]
     left = jnp.concatenate(left, axis=0)
+    which, place = row_of(CH + 2), row_of(CH + 3)
     for half in range(NG // HALF):
-        low = spread(jnp.where(part[CH + 2 : CH + 3] == float(half), part[CH + 3 : CH + 4], -1.0))
+        low = spread(jnp.where(which == float(half), place, -1.0))
         right = [
             jnp.where(low == step + jnp.bfloat16(j), one, none) for j in range(0, HALF, BLOCK)
         ]
@@ -157,12 +157,12 @@
         later[q] = turned(0, LARGE, buffers[q])
 
     def fast(i, width):
-        parts = [later[q, :, :width] for q in range(SIDE)]
         for q in range(SIDE):
+            b = i * SIDE + q
+            block = functools.partial(lambda q, c: later[q, c : c + 1, :width], q)
+            for lanes, sums in products(block, width, table_s[2 * GROUP + 1, b]):
+                emit(b, lanes, sums)
             merge(i + 1, q)
-            b = i * SIDE + q
-            for lanes, sums in products(parts[q], table_s[2 * GROUP + 1, b]):
-                emit(b, lanes, sums)
 
     def slow(b):
         def run(r, target):
@@ -182,7 +182,8 @@
 
         def piece(k, _):
             first = pl.multiple_of(k * LARGE, LARGE)
-            for lanes, sums in products(turned(first, LARGE, packed), size - first):
+            part = turned(first, LARGE, packed)
+            for lanes, sums in products(lambda c: part[c : c + 1], LARGE, size - first):
                 total[:, lanes] += sums
             return 0
 

time: 37.9 us -> 38.4 us (1.013)
  Pallas kernels: 17.1 us -> 17.5 us
    pallas_call x1, Pallas kernels: 14.4 us -> 14.8 us  [per_device(): pl.pallas_call(functools.partial(grid_kernel, 1.0 / math.sqrt(NG), row_bl...]
where the time goes in v19:
time: 38.4 us; the launch traced here: 38.1 us
  blocking collectives  20.6 us (54%)
  Pallas kernels  17.5 us (46%)
    all_to_all x1, blocking collectives, per_device(): lax.all_to_all(own.reshape(runs, ROWS, count), ('tile', 'band'), split_ax...  20.6 us
    pallas_call x1, Pallas kernels, per_device(): pl.pallas_call(functools.partial(grid_kernel, 1.0 / math.sqrt(NG), row_bl...  14.8 us
    pallas_call x1, Pallas kernels, per_device(): pl.pallas_call(functools.partial(run_kernel, cells_dev), out_shape=jax.Sh...  2.71 us

profile of v19, /device:TPU:0, one launch (start us, length us, event | category | flops | bytes accessed | tf_op | source)
XLA Modules:
  0.0 38.1 jit_solution(18316225377875304589)
XLA Ops:
  0.0 2.7 %own_run.1 = bf16[8,4,24,256]{3,2,1,0:T(8,128)(2,1)} custom-call(bf16[96,2048]{1,0:T(8,128)(2,1)} %constant.2.clone.twiddle_ref, bf16[1,256,2048]{2,1,0:T(8,128)(2,1)} %traces_ref.1, s32[1,1024]{1,0:T(1,128)} %bitcast.3, s32[1,1024]{1,0:T(1,128)} %offset_ref.1), custom_call_target="tpu_custom_call" | custom-call | tf_op jit(solution)/shard_map/own_run/pallas_call | solution.py:317
  2.7 20.6 %all_to_all.5.lists_ref = bf16[32,24,256]{2,1,0:T(8,128)(2,1)} all-to-all(bf16[32,24,256]{2,1,0:T(8,128)(2,1)} %bitcast.2), channel_id=1, replica_groups=mesh['band'=4,'tile'=8] {'tile','band'}, dimensions={0} | all-to-all | bytes 786432 | tf_op jit(solution)/shard_map/all_to_all | solution.py:330
  23.3 14.8 %grid.1 = f32[10,2,64,512]{3,2,1,0:T(8,128)} custom-call(bf16[32,24,256]{2,1,0:T(8,128)(2,1)} %all_to_all.5.lists_ref), custom_call_target="tpu_custom_call" | custom-call | tf_op jit(solution)/shard_map/grid/pallas_call | solution.py:352

commit v20 on v16

--- a/solution.py
+++ b/solution.py
@@ -268,7 +268,7 @@
     def sent(f):
         return pltpu.make_async_copy(result.at[f], out_ref.at[f], out_sems.at[f])
 
-    def frequency(f, slot):
+    def form(f, slot):
         for part, p in enumerate((f, FB + f)):
             for i in range(0, NG, TURN):
                 for j in range(0, NG, TURN):
@@ -276,6 +276,8 @@
                     twice[slot, part * NG + i : part * NG + i + TURN, j : j + TURN] = (
                         planes[p, i : i + TURN, j : j + TURN] + across
                     )
+
+    def multiply(f, slot):
         real = twice[slot, pl.ds(first_row, row_block), :]
         imag = twice[slot, pl.ds(NG + first_row, row_block), :]
         own = jnp.concatenate(
@@ -290,8 +292,11 @@
         sent(f).start()
 
     def some(i, _):
+        form(i * BESIDE, 0)
         for q in range(BESIDE):
-            frequency(i * BESIDE + q, q)
+            if q + 1 < BESIDE:
+                form(i * BESIDE + q + 1, q + 1)
+            multiply(i * BESIDE + q, q)
         return 0
 
     lax.fori_loop(0, FB // BESIDE, some, 0)

time: 37.9 us -> 38.2 us (level)
  no operation moved by 1% of the time
where the time goes in v20:
time: 38.2 us; the launch traced here: 38 us
  blocking collectives  20.6 us (54%)
  Pallas kernels  17.4 us (46%)
    all_to_all x1, blocking collectives, per_device(): lax.all_to_all(own.reshape(runs, ROWS, count), ('tile', 'band'), split_ax...  20.6 us
    pallas_call x1, Pallas kernels, per_device(): pl.pallas_call(functools.partial(grid_kernel, 1.0 / math.sqrt(NG), row_bl...  14.7 us
    pallas_call x1, Pallas kernels, per_device(): pl.pallas_call(functools.partial(run_kernel, cells_dev), out_shape=jax.Sh...  2.71 us

profile of v20, /device:TPU:0, one launch (start us, length us, event | category | flops | bytes accessed | tf_op | source)
XLA Modules:
  0.0 38.0 jit_solution(8783821364215155571)
XLA Ops:
  0.0 2.7 %own_run.1 = bf16[8,4,24,256]{3,2,1,0:T(8,128)(2,1)} custom-call(bf16[96,2048]{1,0:T(8,128)(2,1)} %constant.2.clone.twiddle_ref, bf16[1,256,2048]{2,1,0:T(8,128)(2,1)} %traces_ref.1, s32[1,1024]{1,0:T(1,128)} %bitcast.3, s32[1,1024]{1,0:T(1,128)} %offset_ref.1), custom_call_target="tpu_custom_call" | custom-call | tf_op jit(solution)/shard_map/own_run/pallas_call | solution.py:321
  2.7 20.6 %all_to_all.5.lists_ref = bf16[32,24,256]{2,1,0:T(8,128)(2,1)} all-to-all(bf16[32,24,256]{2,1,0:T(8,128)(2,1)} %bitcast.2), channel_id=1, replica_groups=mesh['band'=4,'tile'=8] {'tile','band'}, dimensions={0} | all-to-all | bytes 786432 | tf_op jit(solution)/shard_map/all_to_all | solution.py:334
  23.3 14.7 %grid.1 = f32[10,2,64,512]{3,2,1,0:T(8,128)} custom-call(bf16[32,24,256]{2,1,0:T(8,128)(2,1)} %all_to_all.5.lists_ref), custom_call_target="tpu_custom_call" | custom-call | tf_op jit(solution)/shard_map/grid/pallas_call | solution.py:356

commit v21 on v16

--- a/solution.py
+++ b/solution.py
@@ -21,22 +21,25 @@
 COPY = 32
 WIDTHS = (256, 512, 640)
 LARGE = WIDTHS[-1]
-BESIDE = 5
+BESIDE = 10
+SLOTS = 5
 SIDE = 4
 TURN = 128
 HALF = 256
 VMEM = 56 * 1024 * 1024
 
 
-def twiddle_rows(band_count):
-    time_index = np.arange(NT)[None, None, :]
-    freq_index = np.arange(band_count * FB).reshape(band_count, FB, 1) + 1
+def twiddle_columns(band_count):
+    time_index = np.arange(NT)[:, None, None]
+    freq_index = np.arange(band_count * FB).reshape(1, band_count, FB) + 1
     angle = (time_index * freq_index % NT) * (2.0 * math.pi / NT)
     norm = 1.0 / math.sqrt(NT)
-    table = np.zeros((band_count, ROWS, NT), np.float64)
-    table[:, :FB] = np.cos(angle) * norm
-    table[:, FB:CH] = -np.sin(angle) * norm
-    return table.reshape(band_count * ROWS, NT).astype(ml_dtypes.bfloat16)
+    table = np.zeros((NT, band_count, ROWS), np.float64)
+    table[:, :, :FB] = np.cos(angle) * norm
+    table[:, :, FB:CH] = -np.sin(angle) * norm
+    table = table.reshape(NT, band_count * ROWS)
+    table = np.pad(table, ((0, 0), (0, -band_count * ROWS % 128)))
+    return table.astype(ml_dtypes.bfloat16)
 
 
 def contract_last(left, right):
@@ -67,7 +70,8 @@
     digits = jnp.where(row == CH + 1, source % BLOCK, 0)
     digits = jnp.where(row == CH + 2, receiver // HALF, digits)
     digits = jnp.where(row == CH + 3, receiver % HALF, digits)
-    spectra = contract_last(twiddle_ref[...], traces_ref[0])
+    spectra = jnp.dot(traces_ref[0], twiddle_ref[...], preferred_element_type=jnp.float32)
+    spectra = jnp.transpose(spectra)[: bands * ROWS]
     packed = (spectra + digits.astype(jnp.float32)).astype(jnp.bfloat16)
     ordered = contract_last(packed, permute) + jnp.where(row == CH, starts, 0).astype(jnp.float32)
     for band in range(bands):
@@ -291,7 +295,7 @@
 
     def some(i, _):
         for q in range(BESIDE):
-            frequency(i * BESIDE + q, q)
+            frequency(i * BESIDE + q, q % SLOTS)
         return 0
 
     lax.fori_loop(0, FB // BESIDE, some, 0)
@@ -321,7 +325,7 @@
         compiler_params=params,
         name="own_run",
     )(
-        jnp.asarray(twiddle_rows(band_count)),
+        jnp.asarray(twiddle_columns(band_count)),
         raw_traces,
         bin_owner.reshape(1, length),
         bin_offset,
@@ -337,7 +341,7 @@
         pltpu.VMEM((traces + LARGE, 128), jnp.float32),
         pltpu.VMEM((GROUP, 128), jnp.float32),
         pltpu.VMEM((2 * GROUP + 8, 128), jnp.int32),
-        pltpu.VMEM((BESIDE, 2 * NG, NG), jnp.bfloat16),
+        pltpu.VMEM((SLOTS, 2 * NG, NG), jnp.bfloat16),
         pltpu.VMEM(((CH + 1) * BLOCK, NG), jnp.float32),
         pltpu.VMEM((FB, 2, row_block, NG), jnp.float32),
         pltpu.SMEM((2 * GROUP + 8, 128), jnp.int32),

time: 37.9 us -> 37.7 us (level)
  no operation moved by 1% of the time
where the time goes in v21:
time: 37.7 us; the launch traced here: 37.4 us
  blocking collectives  20.6 us (55%)
  Pallas kernels  16.8 us (45%)
    all_to_all x1, blocking collectives, per_device(): lax.all_to_all(own.reshape(runs, ROWS, count), ('tile', 'band'), split_ax...  20.6 us
    pallas_call x1, Pallas kernels, per_device(): pl.pallas_call(functools.partial(grid_kernel, 1.0 / math.sqrt(NG), row_bl...  14.1 us
    pallas_call x1, Pallas kernels, per_device(): pl.pallas_call(functools.partial(run_kernel, cells_dev), out_shape=jax.Sh...  2.72 us

profile of v21, /device:TPU:0, one launch (start us, length us, event | category | flops | bytes accessed | tf_op | source)
XLA Modules:
  0.0 37.4 jit_solution(7348403748398968658)
XLA Ops:
  0.0 2.7 %own_run.1 = bf16[8,4,24,256]{3,2,1,0:T(8,128)(2,1)} custom-call(bf16[2048,128]{1,0:T(8,128)(2,1)} %constant.2.clone.twiddle_ref, bf16[1,256,2048]{2,1,0:T(8,128)(2,1)} %traces_ref.1, s32[1,1024]{1,0:T(1,128)} %bitcast.3, s32[1,1024]{1,0:T(1,128)} %offset_ref.1), custom_call_target="tpu_custom_call" | custom-call | tf_op jit(solution)/shard_map/own_run/pallas_call | solution.py:320
  2.7 20.6 %all_to_all.5.lists_ref = bf16[32,24,256]{2,1,0:T(8,128)(2,1)} all-to-all(bf16[32,24,256]{2,1,0:T(8,128)(2,1)} %bitcast.2), channel_id=1, replica_groups=mesh['band'=4,'tile'=8] {'tile','band'}, dimensions={0} | all-to-all | bytes 786432 | tf_op jit(solution)/shard_map/all_to_all | solution.py:333
  23.3 14.1 %grid.1 = f32[10,2,64,512]{3,2,1,0:T(8,128)} custom-call(bf16[32,24,256]{2,1,0:T(8,128)(2,1)} %all_to_all.5.lists_ref), custom_call_target="tpu_custom_call" | custom-call | tf_op jit(solution)/shard_map/grid/pallas_call | solution.py:355

commit v22 on v16

--- a/solution.py
+++ b/solution.py
@@ -21,7 +21,8 @@
 COPY = 32
 WIDTHS = (256, 512, 640)
 LARGE = WIDTHS[-1]
-BESIDE = 5
+BESIDE = 10
+SLOTS = 5
 SIDE = 4
 TURN = 128
 HALF = 256
@@ -291,7 +292,7 @@
 
     def some(i, _):
         for q in range(BESIDE):
-            frequency(i * BESIDE + q, q)
+            frequency(i * BESIDE + q, q % SLOTS)
         return 0
 
     lax.fori_loop(0, FB // BESIDE, some, 0)
@@ -337,7 +338,7 @@
         pltpu.VMEM((traces + LARGE, 128), jnp.float32),
         pltpu.VMEM((GROUP, 128), jnp.float32),
         pltpu.VMEM((2 * GROUP + 8, 128), jnp.int32),
-        pltpu.VMEM((BESIDE, 2 * NG, NG), jnp.bfloat16),
+        pltpu.VMEM((SLOTS, 2 * NG, NG), jnp.bfloat16),
         pltpu.VMEM(((CH + 1) * BLOCK, NG), jnp.float32),
         pltpu.VMEM((FB, 2, row_block, NG), jnp.float32),
         pltpu.SMEM((2 * GROUP + 8, 128), jnp.int32),

time: 37.9 us -> 37.8 us (level)
  no operation moved by 1% of the time
where the time goes in v22:
time: 37.8 us; the launch traced here: 37.4 us
  blocking collectives  20.6 us (54%)
  Pallas kernels  16.8 us (44%)
    all_to_all x1, blocking collectives, per_device(): lax.all_to_all(own.reshape(runs, ROWS, count), ('tile', 'band'), split_ax...  20.6 us
    pallas_call x1, Pallas kernels, per_device(): pl.pallas_call(functools.partial(grid_kernel, 1.0 / math.sqrt(NG), row_bl...  14.1 us
    pallas_call x1, Pallas kernels, per_device(): pl.pallas_call(functools.partial(run_kernel, cells_dev), out_shape=jax.Sh...  2.71 us

profile of v22, /device:TPU:0, one launch (start us, length us, event | category | flops | bytes accessed | tf_op | source)
XLA Modules:
  0.0 37.4 jit_solution(15279298039051478858)
XLA Ops:
  0.0 2.7 %own_run.1 = bf16[8,4,24,256]{3,2,1,0:T(8,128)(2,1)} custom-call(bf16[96,2048]{1,0:T(8,128)(2,1)} %constant.2.clone.twiddle_ref, bf16[1,256,2048]{2,1,0:T(8,128)(2,1)} %traces_ref.1, s32[1,1024]{1,0:T(1,128)} %bitcast.3, s32[1,1024]{1,0:T(1,128)} %offset_ref.1), custom_call_target="tpu_custom_call" | custom-call | tf_op jit(solution)/shard_map/own_run/pallas_call | solution.py:317
  2.7 20.6 %all_to_all.5.lists_ref = bf16[32,24,256]{2,1,0:T(8,128)(2,1)} all-to-all(bf16[32,24,256]{2,1,0:T(8,128)(2,1)} %bitcast.2), channel_id=1, replica_groups=mesh['band'=4,'tile'=8] {'tile','band'}, dimensions={0} | all-to-all | bytes 786432 | tf_op jit(solution)/shard_map/all_to_all | solution.py:330
  23.3 14.1 %grid.1 = f32[10,2,64,512]{3,2,1,0:T(8,128)} custom-call(bf16[32,24,256]{2,1,0:T(8,128)(2,1)} %all_to_all.5.lists_ref), custom_call_target="tpu_custom_call" | custom-call | tf_op jit(solution)/shard_map/grid/pallas_call | solution.py:352

commit v23 on v16

--- a/solution.py
+++ b/solution.py
@@ -23,7 +23,7 @@
 LARGE = WIDTHS[-1]
 BESIDE = 5
 SIDE = 4
-TURN = 128
+TURN = 256
 HALF = 256
 VMEM = 56 * 1024 * 1024
 

time: 37.9 us -> 37.7 us (level)
  no operation moved by 1% of the time
where the time goes in v23:
time: 37.7 us; the launch traced here: 37.5 us
  blocking collectives  20.6 us (55%)
  Pallas kernels  16.9 us (45%)
    all_to_all x1, blocking collectives, per_device(): lax.all_to_all(own.reshape(runs, ROWS, count), ('tile', 'band'), split_ax...  20.6 us
    pallas_call x1, Pallas kernels, per_device(): pl.pallas_call(functools.partial(grid_kernel, 1.0 / math.sqrt(NG), row_bl...  14.2 us
    pallas_call x1, Pallas kernels, per_device(): pl.pallas_call(functools.partial(run_kernel, cells_dev), out_shape=jax.Sh...  2.71 us

profile of v23, /device:TPU:0, one launch (start us, length us, event | category | flops | bytes accessed | tf_op | source)
XLA Modules:
  0.0 37.5 jit_solution(13034941965706913539)
XLA Ops:
  0.0 2.7 %own_run.1 = bf16[8,4,24,256]{3,2,1,0:T(8,128)(2,1)} custom-call(bf16[96,2048]{1,0:T(8,128)(2,1)} %constant.2.clone.twiddle_ref, bf16[1,256,2048]{2,1,0:T(8,128)(2,1)} %traces_ref.1, s32[1,1024]{1,0:T(1,128)} %bitcast.3, s32[1,1024]{1,0:T(1,128)} %offset_ref.1), custom_call_target="tpu_custom_call" | custom-call | tf_op jit(solution)/shard_map/own_run/pallas_call | solution.py:316
  2.7 20.6 %all_to_all.5.lists_ref = bf16[32,24,256]{2,1,0:T(8,128)(2,1)} all-to-all(bf16[32,24,256]{2,1,0:T(8,128)(2,1)} %bitcast.2), channel_id=1, replica_groups=mesh['band'=4,'tile'=8] {'tile','band'}, dimensions={0} | all-to-all | bytes 786432 | tf_op jit(solution)/shard_map/all_to_all | solution.py:329
  23.3 14.2 %grid.1 = f32[10,2,64,512]{3,2,1,0:T(8,128)} custom-call(bf16[32,24,256]{2,1,0:T(8,128)(2,1)} %all_to_all.5.lists_ref), custom_call_target="tpu_custom_call" | custom-call | tf_op jit(solution)/shard_map/grid/pallas_call | solution.py:351
